TPU v7x, 128 devices: a whole 4x4x4 slice. The times are simulated.
128 devices in a mesh: occ: 8 (over y, core), vir: 16 (over z, x).
Axes of the slice: x: 4, y: 4, z: 4, core: 2. Of those that a mesh axis runs over, the one named last changes fastest.
Arguments:
- amplitudes: bfloat16 [8, 2, 4096, 4096], P('occ', None, 'vir'), may hold values from -6 to 6
- ladder_ints: bfloat16 [2, 16, 3, 256, 256], P(None, 'vir'), may hold values from -0.21875 to 0.21875
- tile_cols: int32 [16, 3], replicated, may hold values from 0 to 15, as said below
- tile_counts: int32 [16], replicated, may hold values from 1 to 3, as said below
- cycle_ints: bfloat16 [2, 8, 4096], P(None, 'occ', 'vir'), may hold values from -0.375 to 0.375
Outputs:
- residual: bfloat16 [8, 2, 4096, 4096], P('occ', None, 'vir')
Inputs may be any that keep to these rules, and one draw needn't show every extreme that they name: `tile_cols`: in tile row X, slot 0 holds X itself and the 3 slots hold distinct tiles. `tile_counts`: some tile row uses all 3 slots.
All inputs are finite; a program needn't handle non-finite values.
Results may differ from a plain program's by a relative error of at most 0.009.
Values may be sent and summed in bfloat16 or wider, within the bound.
No kernel may reach another device: no remote copies, remote signals or barrier semaphores. Data moves between devices by JAX's collectives and lax.ppermute only.
A program may use at most 192 MiB of HBM per device.

v0:
```python
import jax
import jax.numpy as jnp
from jax import lax
from jax.sharding import PartitionSpec as P


def ladder_from(blocks, int_tiles, tile_cols, partners, tile_rows, tile_count):
    slot_count = tile_cols.shape[1]
    ladder = jnp.zeros((partners, tile_rows, tile_count, tile_rows), jnp.float32)
    for slot_index in range(slot_count):
        picked = jnp.take(blocks, tile_cols[:, slot_index], axis=3)
        ladder = ladder + jnp.einsum(
            "qjaby,qbxy->jabx",
            picked,
            int_tiles[:, :, slot_index],
            preferred_element_type=jnp.float32,
        )
    return ladder


def body(amplitudes, ladder_ints, tile_cols, tile_counts, cycle_ints):
    tile_count, slot_count = tile_cols.shape
    aux_count = ladder_ints.shape[0]
    tile_rows = ladder_ints.shape[3]
    partners = amplitudes.shape[1]
    virtuals = amplitudes.shape[3]
    gathered = lax.all_gather(ladder_ints, "vir", axis=1, tiled=True)
    live_slots = (
        lax.broadcasted_iota(jnp.int32, (tile_count, slot_count), 1) < tile_counts[:, None]
    ).astype(gathered.dtype)
    int_tiles = gathered * live_slots[None, :, :, None, None]
    cycle_local = jnp.einsum(
        "qc,jcb->qjb", cycle_ints[:, 0, :], amplitudes[0], preferred_element_type=jnp.float32
    )
    cycle_total = lax.psum(cycle_local, ("occ", "vir"))
    relaid = lax.all_to_all(amplitudes, "vir", split_axis=3, concat_axis=2, tiled=True)
    items = relaid.shape[1]
    width = relaid.shape[3]
    stacked = relaid.reshape(items, tile_count, tile_rows, width)
    total = jnp.zeros((aux_count, items, tile_count, tile_rows, width), jnp.float32)
    for slot_index in range(slot_count):
        chosen = jnp.take(stacked, tile_cols[:, slot_index], axis=1)
        total = total + jnp.einsum(
            "qaxc,jacd->qjaxd",
            int_tiles[:, :, slot_index],
            chosen,
            preferred_element_type=jnp.float32,
        )
    half_done = lax.all_to_all(
        total.astype(jnp.bfloat16).reshape(aux_count, 1, items, tile_count * tile_rows, width),
        "vir",
        split_axis=3,
        concat_axis=4,
        tiled=True,
    )
    blocks = half_done.reshape(aux_count, partners, tile_rows, tile_count, tile_rows)
    ladder = ladder_from(blocks, int_tiles, tile_cols, partners, tile_rows, tile_count)
    cycle_term = jnp.einsum("qa,qjb->jab", cycle_ints[:, 0, :].astype(jnp.float32), cycle_total)
    summed = ladder.reshape(partners, tile_rows, virtuals) + cycle_term
    return summed.astype(jnp.bfloat16)[None]


def solution(mesh):
    in_specs = (
        P("occ", None, "vir", None),
        P(None, "vir", None, None, None),
        P(),
        P(),
        P(None, "occ", "vir"),
    )
    out_specs = P("occ", None, "vir", None)
    return jax.shard_map(body, mesh=mesh, in_specs=in_specs, out_specs=out_specs, check_vma=False)
```

profile of v0, /device:TPU:0, one launch (start us, length us, event | category | flops | bytes accessed | tf_op | source)
XLA Modules:
  0.0 495.7 jit_solution(14233549953199150290)
XLA Ops:
  6.5 2.1 copy.24
  8.6 0.0 all-gather.2.cloned.1.call-update
  8.6 0.0 copy-start.4
  8.7 0.0 copy-start.5
  8.7 11.1 %copy.25 = bf16[1,2,256,4096]{2,1,0,3:T(2,128)(2,1)} copy(bf16[1,2,256,4096]{3,2,1,0:T(8,128)(2,1)} %param.9) | data formatting | bytes 8388608 | tf_op args[0]
  19.8 8.0 %all-to-all-start = ((bf16[1,2,256,4096]{2,1,0,3:T(2,128)(2,1)}), bf16[1,2,256,4096]{2,1,0,3:T(2,128)(2,1)}, u32[]{:S(2)}, u32[]{:S(2)}) async-start(bf16[1,2,256,4096]{2,1,0,3:T(2,128)(2,1)} %copy.25), calls=%async_computation | async-start | bytes 8388608 | tf_op jit(solution)/shard_map/all_to_all | solution.py:36
  27.9 73.6 %all-to-all-done = bf16[1,2,256,4096]{2,1,0,3:T(2,128)(2,1)} async-done(((bf16[1,2,256,4096]{2,1,0,3:T(2,128)(2,1)}), bf16[1,2,256,4096]{2,1,0,3:T(2,128)(2,1)}, u32[]{:S(2)}, u32[]{:S(2)}) %all-to-all-start) | async-done | bytes 4194336 | tf_op jit(solution)/shard_map/all_to_all | solution.py:36
  101.5 11.1 %copy.27 = bf16[1,2,256,16,256]{4,2,3,1,0:T(8,128)(2,1)} copy(bf16[1,2,256,16,256]{2,1,4,3,0:T(2,128)(2,1)} %bitcast.4) | data formatting | bytes 8388608 | tf_op jit(solution)/shard_map/all_to_all | solution.py:36
  112.6 5.2 %gather_fusion.1 = bf16[16,2,256,256]{3,2,1,0:T(8,128)(2,1)} fusion(bf16[2,16,256,256]{3,2,1,0:T(8,128)(2,1)} %bitcast.131, s32[1024]{0:T(1024)S(1)} %get-tuple-element.18), kind=kCustom, calls=%fused_computation.2.clone | custom fusion | bytes 8388672 | tf_op jit(solution)/shard_map/jit(_take)/gather | solution.py:42
  117.8 5.0 %gather_fusion = bf16[16,2,256,256]{3,2,1,0:T(8,128)(2,1)} fusion(bf16[2,16,256,256]{3,2,1,0:T(8,128)(2,1)} %bitcast.132, s32[1024]{0:T(1024)S(1)} %pad_clamp_fusion.2), kind=kCustom, calls=%fused_computation.clone | custom fusion | bytes 8388672 | tf_op jit(solution)/shard_map/jit(_take)/gather | solution.py:42
  122.8 5.0 %gather_fusion.2 = bf16[16,2,256,256]{3,2,1,0:T(8,128)(2,1)} fusion(bf16[2,16,256,256]{3,2,1,0:T(8,128)(2,1)} %bitcast.133, s32[1024]{0:T(1024)S(1)} %get-tuple-element.17), kind=kCustom, calls=%fused_computation.3.clone | custom fusion | bytes 8388672 | tf_op jit(solution)/shard_map/jit(_take)/gather | solution.py:42
  127.7 21.9 %all-gather.2.cloned.1.call-done = bf16[2,16,3,256,256]{4,3,0,1,2:T(8,128)(2,1)} async-done(((bf16[2,1,3,256,256]{4,3,0,1,2:T(8,128)(2,1)}), bf16[2,16,3,256,256]{4,3,0,1,2:T(8,128)(2,1)}) %all-gather.2.cloned.1.call-update) | async-done | bytes 12582928 | tf_op jit(solution)/shard_map/all_gather | solution.py:27
  149.7 10.9 %broadcast_multiply_fusion = bf16[2,16,3,256,256]{4,3,0,1,2:T(8,128)(2,1)} fusion(bf16[2,16,3,256,256]{4,3,0,1,2:T(8,128)(2,1)} %all-gather.2.cloned.1.call-done, bf16[16,3]{0,1:T(4,128)(2,1)S(1)} %fusion.51), kind=kLoop, calls=%fused_computation.24 | loop fusion | flops 6291456 | bytes 25165920 | tf_op jit(solution)/shard_map/mul | solution.py:31
  160.5 10.6 %fusion.20 = f32[16,2,256,2,256]{2,4,3,1,0:T(8,128)} fusion(bf16[16,2,256,256]{3,2,1,0:T(8,128)(2,1)S(1)} %copy-done.2, pred[16]{0:T(512)(128)(4,1)S(1)} %get-tuple-element.15, bf16[2,16,3,256,256]{4,3,0,1,2:T(8,128)(2,1)} %broadcast_multiply_fusion), kind=kOutput, calls=%fused_computation.31 | convolution fusion | flops 2149580800 | bytes 25165840 | tf_op jit(solution)/shard_map/qaxc,jacd->qjaxd/dot_general | solution.py:43
  171.1 10.4 %fusion.22 = f32[16,2,256,2,256]{2,4,3,1,0:T(8,128)} fusion(bf16[16,2,256,256]{3,2,1,0:T(8,128)(2,1)S(1)} %copy-done.1, pred[16]{0:T(512)(128)(4,1)S(1)} %get-tuple-element.13, bf16[2,16,3,256,256]{4,3,0,1,2:T(8,128)(2,1)} %broadcast_multiply_fusion), kind=kOutput, calls=%fused_computation.33 | convolution fusion | flops 2149580800 | bytes 25165840 | tf_op jit(solution)/shard_map/qaxc,jacd->qjaxd/dot_general | solution.py:43
  181.5 18.3 %fusion.15 = bf16[2,2,16,256,256]{4,3,0,1,2:T(8,128)(2,1)} fusion(f32[16,2,256,2,256]{2,4,3,1,0:T(8,128)} %fusion.22, f32[16,2,256,2,256]{2,4,3,1,0:T(8,128)} %fusion.20, bf16[16,2,256,256]{3,2,1,0:T(8,128)(2,1)} %gather_fusion.2, pred[16]{0:T(512)(128)(4,1)S(1)} %get-tuple-element.6, bf16[2,16,3,256,256]{4,3,0,1,2:T(8,128)(2,1)} %broadcast_multiply_fusion), kind=kOutput, calls=%fused_computation.26 | convolution fusion | flops 2162163712 | bytes 50331664 | tf_op jit(solution)/shard_map/qaxc,jacd->qjaxd/dot_general | solution.py:43
  199.8 7.6 %copy.28 = bf16[2,2,16,256,256]{4,3,2,1,0:T(8,128)(2,1)} copy(bf16[2,2,16,256,256]{4,3,0,1,2:T(8,128)(2,1)} %fusion.15) | data formatting | bytes 16777216 | tf_op jit(solution)/shard_map/convert_element_type | solution.py:50
  207.4 16.4 %copy.29 = bf16[2,1,2,4096,256]{4,2,0,1,3:T(2,128)(2,1)} copy(bf16[2,1,2,4096,256]{4,3,2,0,1:T(8,128)(2,1)} %bitcast.134) | data formatting | bytes 16777216 | tf_op jit(solution)/shard_map/reshape | solution.py:50
  223.8 4.8 all-to-all-start.1
  228.6 2.8 fusion.24
  231.4 177.9 %psum.7 = bf16[2,2,4096]{2,0,1:T(2,128)(2,1)S(1)} all-reduce(f32[2,2,4096]{2,0,1:T(2,128)S(1)} %fusion.24), channel_id=1, replica_groups=mesh['occ'=8,'vir'=16] {'occ','vir'}, use_global_device_ids=true, to_apply=%region_0.3 | all-reduce | flops 16384 | bytes 98304 | tf_op jit(solution)/shard_map/psum | solution.py:35
  409.3 0.0 all-to-all-done.1
  409.3 7.7 %copy.30 = bf16[2,1,2,4096,256]{4,3,2,0,1:T(8,128)(2,1)} copy(bf16[2,1,2,4096,256]{4,2,0,1,3:T(2,128)(2,1)} %all-to-all-done.1) | data formatting | bytes 16777216 | tf_op jit(solution)/shard_map/all_to_all | solution.py:49
  417.0 8.1 %gather_fusion.4 = bf16[16,2,2,256,256]{4,3,2,1,0:T(8,128)(2,1)} fusion(bf16[2,2,256,16,256]{4,2,3,1,0:T(8,128)(2,1)} %bitcast.128, s32[1024]{0:T(1024)S(1)} %get-tuple-element.18), kind=kCustom, calls=%fused_computation.4.clone | custom fusion | bytes 16777280 | tf_op jit(solution)/shard_map/jit(_take)/gather | solution.py:11
  425.1 8.1 %gather_fusion.5 = bf16[16,2,2,256,256]{4,3,2,1,0:T(8,128)(2,1)} fusion(bf16[2,2,256,16,256]{4,2,3,1,0:T(8,128)(2,1)} %bitcast.129, s32[1024]{0:T(1024)S(1)} %get-tuple-element.17), kind=kCustom, calls=%fused_computation.5.clone | custom fusion | bytes 16777280 | tf_op jit(solution)/shard_map/jit(_take)/gather | solution.py:11
  433.2 8.1 %gather_fusion.3 = bf16[16,2,2,256,256]{4,3,2,1,0:T(8,128)(2,1)} fusion(bf16[2,2,256,16,256]{4,2,3,1,0:T(8,128)(2,1)} %bitcast.130, s32[1024]{0:T(1024)S(1)} %pad_clamp_fusion.2), kind=kCustom, calls=%fused_computation.1.clone | custom fusion | bytes 16777280 | tf_op jit(solution)/shard_map/jit(_take)/gather | solution.py:11
  441.3 10.5 %fusion.4 = f32[16,256,2,256,1]{3,1,2,4,0:T(8,128)} fusion(bf16[16,2,2,256,256]{4,3,2,1,0:T(8,128)(2,1)} %gather_fusion.4, pred[16]{0:T(512)(128)(4,1)S(1)} %get-tuple-element.15, bf16[2,16,3,256,256]{4,3,0,1,2:T(8,128)(2,1)} %broadcast_multiply_fusion), kind=kOutput, calls=%fused_computation.14 | convolution fusion | flops 2151677952 | bytes 20971536 | tf_op jit(solution)/shard_map/qjaby,qbxy->jabx/dot_general | solution.py:12
  451.8 7.9 %fusion.2 = f32[16,256,2,256,1]{3,1,2,4,0:T(8,128)} fusion(bf16[16,2,2,256,256]{4,3,2,1,0:T(8,128)(2,1)S(1)} %copy-done.3, pred[16]{0:T(512)(128)(4,1)S(1)} %get-tuple-element.6, bf16[2,16,3,256,256]{4,3,0,1,2:T(8,128)(2,1)} %broadcast_multiply_fusion), kind=kOutput, calls=%fused_computation.12 | convolution fusion | flops 2151677952 | bytes 20971536 | tf_op jit(solution)/shard_map/qjaby,qbxy->jabx/dot_general | solution.py:12
  459.7 15.1 %fusion = f32[2,256,16,256]{1,3,0,2:T(8,128)} fusion(f32[16,256,2,256,1]{3,1,2,4,0:T(8,128)} %fusion.2, f32[16,256,2,256,1]{3,1,2,4,0:T(8,128)} %fusion.4, bf16[16,2,2,256,256]{4,3,2,1,0:T(8,128)(2,1)} %gather_fusion.3, pred[16]{0:T(512)(128)(4,1)S(1)} %get-tuple-element.13, bf16[2,16,3,256,256]{4,3,0,1,2:T(8,128)(2,1)} %broadcast_multiply_fusion), kind=kOutput, calls=%fused_computation.8 | convolution fusion | flops 2155872256 | bytes 37748752 | tf_op jit(solution)/shard_map/qjaby,qbxy->jabx/dot_general | solution.py:12
  474.8 3.9 copy.34
  478.8 3.8 fusion.14
  482.5 6.3 %copy.35 = bf16[1,2,256,4096]{3,2,1,0:T(8,128)(2,1)} copy(bf16[1,2,256,4096]{2,3,1,0:T(8,128)(2,1)} %fusion.14) | data formatting | bytes 8388608 | tf_op jit(solution)/shard_map/broadcast_in_dim | solution.py:60
  (15 shorter events, 0.1 us)
Async XLA Ops:
  6.5 222.0 %copy-start = (bf16[2,1,256]{2,0,1:T(2,128)(2,1)S(1)}, bf16[2,1,256]{2,0,1:T(2,128)(2,1)}, u32[]{:S(2)}) copy-start(bf16[2,1,256]{2,0,1:T(2,128)(2,1)} %param.13) | copy-start | bytes 3076
  6.5 143.1 %all-gather.2.cloned.1.call-start = ((), (), s32[]{:S(2)}) async-start(), calls=%async_computation.2 | async-start | bytes 13369344 | tf_op jit(solution)/shard_map/all_gather | solution.py:27
  8.6 19.2 %copy-start.4 = (s32[16,3]{0,1:T(4,128)S(1)}, s32[16,3]{0,1:T(4,128)}, u32[]{:S(2)}) copy-start(s32[16,3]{0,1:T(4,128)} %param.11) | copy-start | bytes 580
  8.7 19.2 %copy-start.5 = (s32[16]{0:T(128)S(1)}, s32[16]{0:T(128)}, u32[]{:S(2)}) copy-start(s32[16]{0:T(128)} %param.12) | copy-start | bytes 196
  19.8 81.7 %all-to-all-start = ((bf16[1,2,256,4096]{2,1,0,3:T(2,128)(2,1)}), bf16[1,2,256,4096]{2,1,0,3:T(2,128)(2,1)}, u32[]{:S(2)}, u32[]{:S(2)}) async-start(bf16[1,2,256,4096]{2,1,0,3:T(2,128)(2,1)} %copy.25), calls=%async_computation | async-start | bytes 8388608 | tf_op jit(solution)/shard_map/all_to_all | solution.py:36
  149.7 10.9 %copy-start.2 = (bf16[16,2,256,256]{3,2,1,0:T(8,128)(2,1)S(1)}, bf16[16,2,256,256]{3,2,1,0:T(8,128)(2,1)}, u32[]{:S(2)}) copy-start(bf16[16,2,256,256]{3,2,1,0:T(8,128)(2,1)} %gather_fusion.1) | copy-start | bytes 12582916
  160.5 10.6 %copy-start.1 = (bf16[16,2,256,256]{3,2,1,0:T(8,128)(2,1)S(1)}, bf16[16,2,256,256]{3,2,1,0:T(8,128)(2,1)}, u32[]{:S(2)}) copy-start(bf16[16,2,256,256]{3,2,1,0:T(8,128)(2,1)} %gather_fusion) | copy-start | bytes 12582916
  223.8 185.5 %all-to-all-start.1 = ((bf16[2,1,2,4096,256]{4,2,0,1,3:T(2,128)(2,1)}), bf16[2,1,2,4096,256]{4,2,0,1,3:T(2,128)(2,1)}, u32[]{:S(2)}, u32[]{:S(2)}) async-start(bf16[2,1,2,4096,256]{4,2,0,1,3:T(2,128)(2,1)} %copy.29), calls=%async_computation.1 | async-start | bytes 16777216 | tf_op jit(solution)/shard_map/all_to_all | solution.py:49
  441.3 10.5 %copy-start.3 = (bf16[16,2,2,256,256]{4,3,2,1,0:T(8,128)(2,1)S(1)}, bf16[16,2,2,256,256]{4,3,2,1,0:T(8,128)(2,1)}, u32[]{:S(2)}) copy-start(bf16[16,2,2,256,256]{4,3,2,1,0:T(8,128)(2,1)} %gather_fusion.5) | copy-start | bytes 25165828
Sparse Core Ops, SparseCore 0:
  9.5 140.1 all-gather.1
where the time goes:
time: 498 us; the launch traced here: 496 us
  blocking collectives  178 us (36%)
  local copies, waits for them, and re-layouts  106 us (21%)
  waiting for transfers between devices  95.5 us (19%)
  matrix products  79.4 us (16%)
  between operations  13.5 us (3%)
  starting transfers between devices  12.8 us (3%)
  other arithmetic  10.9 us (2%)
    psum x1, blocking collectives, body(): cycle_total = lax.psum(cycle_local, ('occ', 'vir'))  178 us
    all_to_all x1, waiting for transfers between devices, body(): lax.all_to_all(amplitudes, 'vir', split_axis=3, concat_axis=2, tiled=True)  73.6 us
    dot_general x3, matrix products, body(): jnp.einsum('qaxc,jacd->qjaxd', int_tiles[:, :, slot_index], chosen, prefe...  39.3 us
    dot_general x3, matrix products, ladder_from(): jnp.einsum('qjaby,qbxy->jabx', picked, int_tiles[:, :, slot_index], prefe...  33.5 us
    gather x3, local copies, waits for them, and re-layouts, ladder_from(): picked = jnp.take(blocks, tile_cols[:, slot_index], axis=3)  24.4 us
    all_gather x1, waiting for transfers between devices, body(): gathered = lax.all_gather(ladder_ints, 'vir', axis=1, tiled=True)  21.9 us
    reshape x1, local copies, waits for them, and re-layouts, body(): total.astype(jnp.bfloat16)  16.4 us
    gather x3, local copies, waits for them, and re-layouts, body(): chosen = jnp.take(stacked, tile_cols[:, slot_index], axis=1)  15.1 us
  transfers between devices with their start and end apart: 3, of which 2 were waited for; matrix products, arithmetic and copies ran while one was open for 8% of the time, Pallas kernels for 0%

commit v1 on v0

v1 whole, which is shorter than its diff:
```python
import jax
import jax.numpy as jnp
from jax import lax
from jax.experimental import pallas as pl
from jax.experimental.pallas import tpu as pltpu
from jax.sharding import PartitionSpec as P

TILE = 256
SLOTS = 3
AUX = 2
WIDE = 1024
ROWS_PER_STEP = 2


def ladder_kernel(
    partner, parts, cols_ref, counts_ref, own_ref, t0_ref, t1_ref, t2_ref, ints_ref, cycle_ref, left_ref, out_ref, half_ref
):
    tile_count = counts_ref.shape[0]
    step = pl.program_id(0)
    first_steps = tile_count * TILE // WIDE
    per_step = WIDE // TILE

    @pl.when(step < first_steps)
    def _():
        for piece in range(per_step):
            span = slice(piece * TILE, (piece + 1) * TILE)
            total = jnp.dot(own_ref[0], t0_ref[:, span], preferred_element_type=jnp.float32)
            total += jnp.dot(own_ref[1], t1_ref[:, span], preferred_element_type=jnp.float32)
            total += jnp.dot(own_ref[2], t2_ref[:, span], preferred_element_type=jnp.float32)
            half_ref[step * per_step + piece] = total.reshape(AUX, TILE, TILE).astype(jnp.bfloat16)

    @pl.when(step >= first_steps)
    def _():
        part_rows = AUX * SLOTS * TILE // parts
        for piece in range(ROWS_PER_STEP):
            row = (step - first_steps) * ROWS_PER_STEP + piece
            count = counts_ref[row]
            for slots in range(1, SLOTS + 1):

                @pl.when(count == slots)
                def _(slots=slots, piece=piece, row=row):
                    ints = ints_ref[:, piece * part_rows : (piece + 1) * part_rows, :].reshape(AUX * SLOTS * TILE, TILE)
                    total = jnp.zeros((TILE, TILE), jnp.float32)
                    for slot in range(slots):
                        half = half_ref[cols_ref[row * SLOTS + slot]]
                        for aux in range(AUX):
                            at = (aux * SLOTS + slot) * TILE
                            total += lax.dot_general(
                                half[aux],
                                ints[at : at + TILE],
                                (((1,), (1,)), ((), ())),
                                preferred_element_type=jnp.float32,
                            )
                    for aux in range(AUX):
                        line = (aux * 2 + partner) * tile_count + row
                        total += left_ref[:, aux : aux + 1] * cycle_ref[pl.ds(line, 1), :]
                    out_ref[:, piece * TILE : (piece + 1) * TILE] = total.astype(jnp.bfloat16)


def ladder(partner, parts, cols, counts, own, rows, ints, cycle, left):
    tile_count = counts.shape[0]
    first_steps = tile_count * TILE // WIDE
    last_steps = tile_count // ROWS_PER_STEP
    part_rows = AUX * SLOTS * TILE // parts
    row_spec = pl.BlockSpec((TILE, WIDE), lambda g, *_: (0, jnp.minimum(g, first_steps - 1)))
    whole = lambda shape: pl.BlockSpec(shape, lambda g, *_: (0,) * len(shape))
    return pl.pallas_call(
        lambda *refs: ladder_kernel(partner, parts, *refs),
        grid_spec=pltpu.PrefetchScalarGridSpec(
            num_scalar_prefetch=2,
            grid=(first_steps + last_steps,),
            in_specs=[
                whole((SLOTS, AUX * TILE, TILE)),
                row_spec,
                row_spec,
                row_spec,
                pl.BlockSpec((parts, ROWS_PER_STEP * part_rows, TILE), lambda g, *_: (0, jnp.maximum(g - first_steps, 0), 0)),
                whole(cycle.shape),
                whole(left.shape),
            ],
            out_specs=pl.BlockSpec((TILE, ROWS_PER_STEP * TILE), lambda g, *_: (0, jnp.maximum(g - first_steps, 0))),
            scratch_shapes=[pltpu.VMEM((tile_count, AUX, TILE, TILE), jnp.bfloat16)],
        ),
        out_shape=jax.ShapeDtypeStruct((TILE, tile_count * TILE), jnp.bfloat16),
        compiler_params=pltpu.CompilerParams(vmem_limit_bytes=40 * 1024 * 1024),
        cost_estimate=pl.CostEstimate(flops=6 * 10**9, bytes_accessed=20 * 2**20, transcendentals=0),
    )(cols, counts, own, *rows, ints, cycle, left)


def body(amplitudes, ladder_ints, tile_cols, tile_counts, cycle_ints):
    tile_count = tile_cols.shape[0]
    partners = amplitudes.shape[1]
    virtuals = amplitudes.shape[3]
    parts = lax.axis_size("occ")
    amps = amplitudes[0]

    part_rows = AUX * SLOTS * TILE // parts
    flat_ints = ladder_ints.reshape(AUX * SLOTS * TILE, TILE)
    own_part = lax.dynamic_slice_in_dim(flat_ints, lax.axis_index("occ") * part_rows, part_rows, axis=0)
    left = cycle_ints[:, 0, :]
    cycle_local = jnp.einsum("qc,jcb->qjb", left, amps, preferred_element_type=jnp.float32)
    lines = AUX * partners * tile_count
    payload = jnp.concatenate([own_part, cycle_local.astype(jnp.bfloat16).reshape(lines, TILE)])
    over_vir = lax.all_gather(payload, "vir", axis=0)
    cycle_vir = jnp.sum(over_vir[:, part_rows:].astype(jnp.float32), axis=0).astype(jnp.bfloat16)
    payload = jnp.concatenate([over_vir[:, :part_rows].reshape(tile_count * part_rows, TILE), cycle_vir])
    ints = lax.all_gather(payload, "occ", axis=0)
    cycle = jnp.sum(ints[:, tile_count * part_rows :].astype(jnp.float32), axis=0)

    me = lax.axis_index("vir")
    live = (jnp.arange(SLOTS) < tile_counts[me]).astype(jnp.bfloat16)
    own = (ladder_ints[:, 0] * live[None, :, None, None]).transpose(1, 0, 2, 3).reshape(SLOTS, AUX * TILE, TILE)

    cols = tile_cols.reshape(-1)
    left = left.astype(jnp.float32).T

    spread = []
    for partner in range(partners):
        chunks = amps[partner].reshape(tile_count, TILE // tile_count, virtuals)
        spread.append(lax.all_to_all(chunks, "vir", split_axis=0, concat_axis=0, tiled=True))
    outs = []
    for partner in range(partners):
        rows = [amps[partner]]
        for slot in range(1, SLOTS):
            picked = jnp.take(spread[partner], tile_cols[:, slot], axis=0, mode="clip")
            fetched = lax.all_to_all(picked, "vir", split_axis=0, concat_axis=0, tiled=True)
            rows.append(fetched.reshape(TILE, virtuals))
        outs.append(ladder(partner, parts, cols, tile_counts, own, rows, ints, cycle, left))
    return jnp.stack(outs)[None]


def solution(mesh):
    in_specs = (
        P("occ", None, "vir", None),
        P(None, "vir", None, None, None),
        P(),
        P(),
        P(None, "occ", "vir"),
    )
    out_specs = P("occ", None, "vir", None)
    return jax.shard_map(body, mesh=mesh, in_specs=in_specs, out_specs=out_specs, check_vma=False)
```

time: 498 us -> 296 us (0.59)
  blocking collectives: 178 us -> 32.6 us
  local copies, waits for them, and re-layouts: 106 us -> 28.5 us
  matrix products: 79.4 us -> 2.93 us
  waiting for transfers between devices: 95.5 us -> 158 us
  Pallas kernels: 0 us -> 30.8 us
  starting transfers between devices: 12.8 us -> 20.9 us
    psum x1 -> x0, blocking collectives: 178 us -> none  [body(): cycle_total = lax.psum(cycle_local, ('occ', 'vir'))]
    dot_general x8 -> x1, matrix products: 79.4 us -> 2.93 us  [body(): jnp.einsum('qc,jcb->qjb', left, amps, preferred_element_type=jnp.float32)]
    all_to_all x2 -> x5, waiting for transfers between devices: 73.6 us -> 110 us  [the longest x4 85.6 us: body(): lax.all_to_all(picked, 'vir', split_axis=0, concat_axis=0, tiled=True)]
    all_to_all x0 -> x1, blocking collectives: none -> 32.6 us  [body(): lax.all_to_all(chunks, 'vir', split_axis=0, concat_axis=0, tiled=True)]
    pallas_call x0 -> x2, Pallas kernels: none -> 30.8 us  [ladder(): pl.pallas_call(lambda *refs: ladder_kernel(partner, parts, *refs), grid_s...]
    all_gather x1 -> x2, waiting for transfers between devices: 21.9 us -> 47.9 us  [the longest x1 47.8 us: body(): over_vir = lax.all_gather(payload, 'vir', axis=0)]
    gather x6 -> x4, local copies, waits for them, and re-layouts: 39.5 us -> 14.6 us  [body(): picked = jnp.take(spread[partner], tile_cols[:, slot], axis=0, mode='clip')]
    all_to_all x2 -> x0, local copies, waits for them, and re-layouts: 18.8 us -> none  [the longest x1 11.1 us: body(): lax.all_to_all(amplitudes, 'vir', split_axis=3, concat_axis=2, tiled=True)]
  transfers between devices with their start and end apart: 3 -> 7, of which waited for: 2 -> 6; matrix products, arithmetic and copies ran while one was open for 8% -> 8% of each run, Pallas kernels for 0% -> 5%
where the time goes in v1:
time: 296 us; the launch traced here: 295 us
  waiting for transfers between devices  158 us (53%)
  blocking collectives  32.6 us (11%)
  Pallas kernels  30.8 us (10%)
  local copies, waits for them, and re-layouts  28.5 us (10%)
  starting transfers between devices  20.9 us (7%)
  between operations  13.6 us (5%)
  other arithmetic  7.23 us (2%)
    all_to_all x4, waiting for transfers between devices, body(): lax.all_to_all(picked, 'vir', split_axis=0, concat_axis=0, tiled=True)  85.6 us
    all_gather x1, waiting for transfers between devices, body(): over_vir = lax.all_gather(payload, 'vir', axis=0)  47.8 us
    all_to_all x1, blocking collectives, body(): lax.all_to_all(chunks, 'vir', split_axis=0, concat_axis=0, tiled=True)  32.6 us
    pallas_call x2, Pallas kernels, ladder(): pl.pallas_call(lambda *refs: ladder_kernel(partner, parts, *refs), grid_s...  30.8 us
    all_to_all x1, waiting for transfers between devices, body(): lax.all_to_all(chunks, 'vir', split_axis=0, concat_axis=0, tiled=True)  24.5 us
    all_to_all x4, starting transfers between devices, body(): lax.all_to_all(picked, 'vir', split_axis=0, concat_axis=0, tiled=True)  17 us
    gather x4, local copies, waits for them, and re-layouts, body(): picked = jnp.take(spread[partner], tile_cols[:, slot], axis=0, mode='clip')  14.6 us
    unnamed x20, local copies, waits for them, and re-layouts  6.07 us
  transfers between devices with their start and end apart: 7, of which 6 were waited for; matrix products, arithmetic and copies ran while one was open for 8% of the time, Pallas kernels for 5%

profile of v1, /device:TPU:0, one launch (start us, length us, event | category | flops | bytes accessed | tf_op | source)
XLA Modules:
  0.0 294.7 jit_solution(5654682152977913131)
XLA Ops:
  6.5 2.9 convolution_convert_fusion
  9.6 0.7 pad_maximum_fusion.1
  10.3 47.8 %all-gather.5.cloned.1.call-done = bf16[4096,256]{1,0:T(8,128)(2,1)} async-done(((bf16[256,256]{1,0:T(8,128)(2,1)}), bf16[4096,256]{1,0:T(8,128)(2,1)}) %all-gather.5.cloned.1.call-update) | async-done | bytes 2097168 | tf_op jit(solution)/shard_map/all_gather | solution.py:104
  58.2 1.5 slice.42
  59.7 1.1 slice_reduce_fusion
  60.8 1.3 pad_maximum_fusion
  62.1 5.4 %fusion.3 = (bf16[1,1,256,4096]{3,2,1,0:T(8,128)(2,1)S(1)}, bf16[256,4096]{1,0:T(8,128)(2,1)}, bf16[256,4096]{1,0:T(8,128)(2,1)}, bf16[1,1,256,4096]{3,2,1,0:T(8,128)(2,1)}) fusion(bf16[1,2,256,4096]{3,2,1,0:T(8,128)(2,1)} %param.5), kind=kLoop, calls=%fused_computation.23 | loop fusion | bytes 12582912 | tf_op jit(solution)/shard_map/slice | solution.py:123
  67.5 32.6 %all_to_all.30 = bf16[16,16,4096]{2,1,0:T(8,128)(2,1)} all-to-all(bf16[16,16,4096]{2,1,0:T(8,128)(2,1)S(1)} %bitcast.51), channel_id=1, replica_groups=mesh['occ'=8,'vir'=16] {'vir'}, dimensions={0} | all-to-all | bytes 4194304 | tf_op jit(solution)/shard_map/all_to_all | solution.py:120
  100.2 3.8 %all-to-all-start.3 = ((bf16[16,16,4096]{2,1,0:T(8,128)(2,1)}), bf16[16,16,4096]{2,1,0:T(8,128)(2,1)S(1)}, u32[]{:S(2)}, u32[]{:S(2)}) async-start(bf16[16,16,4096]{2,1,0:T(8,128)(2,1)} %bitcast.50), calls=%async_computation.3 | async-start | bytes 4194304 | tf_op jit(solution)/shard_map/all_to_all | solution.py:120
  104.0 3.7 %gather_fusion = bf16[16,16,4096]{2,1,0:T(8,128)(2,1)} fusion(bf16[16,16,4096]{2,1,0:T(8,128)(2,1)} %all_to_all.30, s32[1024]{0:T(1024)S(1)} %pad_clamp_fusion.1), kind=kCustom, calls=%fused_computation | custom fusion | bytes 4194368 | tf_op jit(solution)/shard_map/jit(_take)/gather | solution.py:125
  107.7 24.5 %all-to-all-done.3 = bf16[16,16,4096]{2,1,0:T(8,128)(2,1)S(1)} async-done(((bf16[16,16,4096]{2,1,0:T(8,128)(2,1)}), bf16[16,16,4096]{2,1,0:T(8,128)(2,1)S(1)}, u32[]{:S(2)}, u32[]{:S(2)}) %all-to-all-start.3) | async-done | bytes 2097184 | tf_op jit(solution)/shard_map/all_to_all | solution.py:120
  132.3 1.3 copy-done.5
  133.6 3.7 %all-to-all-start.1 = ((bf16[16,16,4096]{2,1,0:T(8,128)(2,1)}), bf16[16,16,4096]{2,1,0:T(8,128)(2,1)S(1)}, u32[]{:S(2)}, u32[]{:S(2)}) async-start(bf16[16,16,4096]{2,1,0:T(8,128)(2,1)} %gather_fusion), calls=%async_computation.1 | async-start | bytes 4194304 | tf_op jit(solution)/shard_map/all_to_all | solution.py:126
  137.3 3.6 %gather_fusion.1 = bf16[16,16,4096]{2,1,0:T(8,128)(2,1)} fusion(bf16[16,16,4096]{2,1,0:T(8,128)(2,1)} %all_to_all.30, s32[1024]{0:T(1024)S(1)} %pad_clamp_fusion), kind=kCustom, calls=%fused_computation.1 | custom fusion | bytes 4194368 | tf_op jit(solution)/shard_map/jit(_take)/gather | solution.py:125
  141.0 26.1 %all-to-all-done.1 = bf16[16,16,4096]{2,1,0:T(8,128)(2,1)S(1)} async-done(((bf16[16,16,4096]{2,1,0:T(8,128)(2,1)}), bf16[16,16,4096]{2,1,0:T(8,128)(2,1)S(1)}, u32[]{:S(2)}, u32[]{:S(2)}) %all-to-all-start.1) | async-done | bytes 2097184 | tf_op jit(solution)/shard_map/all_to_all | solution.py:126
  167.1 4.4 %all-to-all-start.2 = ((bf16[16,16,4096]{2,1,0:T(8,128)(2,1)}), bf16[16,16,4096]{2,1,0:T(8,128)(2,1)}, u32[]{:S(2)}, u32[]{:S(2)}) async-start(bf16[16,16,4096]{2,1,0:T(8,128)(2,1)} %gather_fusion.1), calls=%async_computation.2 | async-start | bytes 4194304 | tf_op jit(solution)/shard_map/all_to_all | solution.py:126
  171.5 3.7 %gather_fusion.2 = bf16[16,16,4096]{2,1,0:T(8,128)(2,1)} fusion(bf16[16,16,4096]{2,1,0:T(8,128)(2,1)} %copy-done.5, s32[1024]{0:T(1024)S(1)} %pad_clamp_fusion.1), kind=kCustom, calls=%fused_computation.2 | custom fusion | bytes 4194368 | tf_op jit(solution)/shard_map/jit(_take)/gather | solution.py:125
  175.2 25.5 %all-to-all-done.2 = bf16[16,16,4096]{2,1,0:T(8,128)(2,1)} async-done(((bf16[16,16,4096]{2,1,0:T(8,128)(2,1)}), bf16[16,16,4096]{2,1,0:T(8,128)(2,1)}, u32[]{:S(2)}, u32[]{:S(2)}) %all-to-all-start.2) | async-done | bytes 2097184 | tf_op jit(solution)/shard_map/all_to_all | solution.py:126
  200.7 4.4 %all-to-all-start.4 = ((bf16[16,16,4096]{2,1,0:T(8,128)(2,1)}), bf16[16,16,4096]{2,1,0:T(8,128)(2,1)}, u32[]{:S(2)}, u32[]{:S(2)}) async-start(bf16[16,16,4096]{2,1,0:T(8,128)(2,1)} %gather_fusion.2), calls=%async_computation.4 | async-start | bytes 4194304 | tf_op jit(solution)/shard_map/all_to_all | solution.py:126
  205.2 3.6 %gather_fusion.3 = bf16[16,16,4096]{2,1,0:T(8,128)(2,1)} fusion(bf16[16,16,4096]{2,1,0:T(8,128)(2,1)} %copy-done.5, s32[1024]{0:T(1024)S(1)} %pad_clamp_fusion), kind=kCustom, calls=%fused_computation.3 | custom fusion | bytes 4194368 | tf_op jit(solution)/shard_map/jit(_take)/gather | solution.py:125
  208.8 25.7 %all-to-all-done.4 = bf16[16,16,4096]{2,1,0:T(8,128)(2,1)} async-done(((bf16[16,16,4096]{2,1,0:T(8,128)(2,1)}), bf16[16,16,4096]{2,1,0:T(8,128)(2,1)}, u32[]{:S(2)}, u32[]{:S(2)}) %all-to-all-start.4) | async-done | bytes 2097184 | tf_op jit(solution)/shard_map/all_to_all | solution.py:126
  234.6 4.5 %all-to-all-start.5 = ((bf16[16,16,4096]{2,1,0:T(8,128)(2,1)}), bf16[16,16,4096]{2,1,0:T(8,128)(2,1)}, u32[]{:S(2)}, u32[]{:S(2)}) async-start(bf16[16,16,4096]{2,1,0:T(8,128)(2,1)} %gather_fusion.3), calls=%async_computation.5 | async-start | bytes 4194304 | tf_op jit(solution)/shard_map/all_to_all | solution.py:126
  239.3 0.6 dynamic_slice.6
  239.9 0.6 compare_convert_fusion
  240.8 1.0 convert_reduce_fusion.refs_7_
  241.9 1.6 copy-done.1
  243.4 15.3 %shard_map.55 = bf16[256,4096]{1,0:T(8,128)(2,1)S(1)} custom-call(s32[48]{0:T(128)S(1)} %reshape.38.refs_0_, s32[16]{0:T(128)S(1)} %copy-done.4, bf16[3,512,256]{2,1,0:T(8,128)(2,1)S(1)} %bitcast.45, bf16[256,4096]{1,0:T(8,128)(2,1)S(1)} %copy-done.1, bf16[256,4096]{1,0:T(8,128)(2,1)S(1)} %bitcast.42, bf16[256,4096]{1,0:T(8,128)(2,1)} %bitcast.9.refs_5_, ...), custom_call_target="tpu_custom_call" | custom-call | flops 6000000000 | bytes 20971520 | tf_op jit(solution)/shard_map/pallas_call | solution.py:67
  258.7 1.3 copy-done.2
  260.0 8.2 %all-to-all-done.5 = bf16[16,16,4096]{2,1,0:T(8,128)(2,1)} async-done(((bf16[16,16,4096]{2,1,0:T(8,128)(2,1)}), bf16[16,16,4096]{2,1,0:T(8,128)(2,1)}, u32[]{:S(2)}, u32[]{:S(2)}) %all-to-all-start.5) | async-done | bytes 2097184 | tf_op jit(solution)/shard_map/all_to_all | solution.py:126
  268.3 1.6 copy-done
  269.9 15.6 %shard_map.56 = bf16[256,4096]{1,0:T(8,128)(2,1)S(1)} custom-call(s32[48]{0:T(128)S(1)} %reshape.38.refs_0_, s32[16]{0:T(128)S(1)} %copy-done.4, bf16[3,512,256]{2,1,0:T(8,128)(2,1)S(1)} %bitcast.46, bf16[256,4096]{1,0:T(8,128)(2,1)S(1)} %copy-done, bf16[256,4096]{1,0:T(8,128)(2,1)} %bitcast.21.refs_4_, bf16[256,4096]{1,0:T(8,128)(2,1)} %bitcast.22.refs_5_, ...), custom_call_target="tpu_custom_call" | custom-call | flops 6000000000 | bytes 20971520 | tf_op jit(solution)/shard_map/pallas_call | solution.py:67
  285.4 2.4 maximum_bitcast_fusion
  (31 shorter events, 0.7 us)
Async XLA Ops:
  6.5 51.6 %all-gather.5.cloned.1.call-start = ((), (), s32[]{:S(2)}) async-start(), calls=%async_computation.6 | async-start | bytes 2228224 | tf_op jit(solution)/shard_map/all_gather | solution.py:104
  6.5 3.0 %copy-start.6 = (bf16[2,1,3,256,256]{4,3,2,1,0:T(8,128)(2,1)S(1)}, bf16[2,1,3,256,256]{4,3,2,1,0:T(8,128)(2,1)}, u32[]{:S(2)}) copy-start(bf16[2,1,3,256,256]{4,3,2,1,0:T(8,128)(2,1)} %param.6) | copy-start | bytes 2359300
  10.3 230.6 %all-gather.7.cloned.1.call-start = ((), (), s32[]{:S(2)}) async-start(), calls=%async_computation.7 | async-start | bytes 14450688 | tf_op jit(solution)/shard_map/all_gather | solution.py:107
  100.2 3.9 %copy-start.7 = (s32[16,3]{0,1:T(4,128)S(1)}, s32[16,3]{0,1:T(4,128)}, u32[]{:S(2)}) copy-start(s32[16,3]{0,1:T(4,128)} %param.7) | copy-start | bytes 580
  100.2 32.1 %all-to-all-start.3 = ((bf16[16,16,4096]{2,1,0:T(8,128)(2,1)}), bf16[16,16,4096]{2,1,0:T(8,128)(2,1)S(1)}, u32[]{:S(2)}, u32[]{:S(2)}) async-start(bf16[16,16,4096]{2,1,0:T(8,128)(2,1)} %bitcast.50), calls=%async_computation.3 | async-start | bytes 4194304 | tf_op jit(solution)/shard_map/all_to_all | solution.py:120
  132.3 1.3 copy-start.5
  133.6 33.5 %all-to-all-start.1 = ((bf16[16,16,4096]{2,1,0:T(8,128)(2,1)}), bf16[16,16,4096]{2,1,0:T(8,128)(2,1)S(1)}, u32[]{:S(2)}, u32[]{:S(2)}) async-start(bf16[16,16,4096]{2,1,0:T(8,128)(2,1)} %gather_fusion), calls=%async_computation.1 | async-start | bytes 4194304 | tf_op jit(solution)/shard_map/all_to_all | solution.py:126
  167.1 33.6 %all-to-all-start.2 = ((bf16[16,16,4096]{2,1,0:T(8,128)(2,1)}), bf16[16,16,4096]{2,1,0:T(8,128)(2,1)}, u32[]{:S(2)}, u32[]{:S(2)}) async-start(bf16[16,16,4096]{2,1,0:T(8,128)(2,1)} %gather_fusion.1), calls=%async_computation.2 | async-start | bytes 4194304 | tf_op jit(solution)/shard_map/all_to_all | solution.py:126
  200.7 33.8 %all-to-all-start.4 = ((bf16[16,16,4096]{2,1,0:T(8,128)(2,1)}), bf16[16,16,4096]{2,1,0:T(8,128)(2,1)}, u32[]{:S(2)}, u32[]{:S(2)}) async-start(bf16[16,16,4096]{2,1,0:T(8,128)(2,1)} %gather_fusion.2), calls=%async_computation.4 | async-start | bytes 4194304 | tf_op jit(solution)/shard_map/all_to_all | solution.py:126
  208.8 30.2 %copy-start.8 = (bf16[2,1,256]{2,0,1:T(2,128)(2,1)S(1)}, bf16[2,1,256]{2,0,1:T(2,128)(2,1)}, u32[]{:S(2)}) copy-start(bf16[2,1,256]{2,0,1:T(2,128)(2,1)} %param.9) | copy-start | bytes 3076
  208.8 30.4 %copy-start.4 = (s32[16]{0:T(128)S(1)}, s32[16]{0:T(128)}, u32[]{:S(2)}) copy-start(s32[16]{0:T(128)} %refs_1_.3) | copy-start | bytes 196
  234.6 33.7 %all-to-all-start.5 = ((bf16[16,16,4096]{2,1,0:T(8,128)(2,1)}), bf16[16,16,4096]{2,1,0:T(8,128)(2,1)}, u32[]{:S(2)}, u32[]{:S(2)}) async-start(bf16[16,16,4096]{2,1,0:T(8,128)(2,1)} %gather_fusion.3), calls=%async_computation.5 | async-start | bytes 4194304 | tf_op jit(solution)/shard_map/all_to_all | solution.py:126
  241.8 1.6 copy-start.1
  258.7 1.3 copy-start.2
  268.3 1.6 copy-start
  269.9 15.6 %copy-start.3 = (bf16[256,4096]{1,0:T(8,128)(2,1)S(1)}, bf16[256,4096]{1,0:T(8,128)(2,1)}, u32[]{:S(2)}) copy-start(bf16[256,4096]{1,0:T(8,128)(2,1)} %copy-done.2) | copy-start | bytes 6291460
Sparse Core Ops, SparseCore 0:
  10.4 47.7 all-gather.4
  62.2 67.7 all-gather.6

commit v2 on v0

v2 whole, which is shorter than its diff:
```python
import functools

import jax
import jax.numpy as jnp
from jax import lax
from jax.experimental import pallas as pl
from jax.experimental.pallas import tpu as pltpu
from jax.sharding import PartitionSpec as P

ROW_CHUNKS = 4
INT_CHUNKS = 8
EXTRA = 16
MIB = 2**20
HBM = pl.BlockSpec(memory_space=pltpu.HBM)
VMEM = pl.BlockSpec(memory_space=pltpu.VMEM)
SMEM = pl.BlockSpec(memory_space=pltpu.SMEM)


def pairs(total, count):
    values = total[..., :count, :]
    rest = values - values.astype(jnp.bfloat16).astype(jnp.float32)
    empty = jnp.zeros(values.shape[:-2] + (EXTRA - 2 * count, values.shape[-1]), jnp.float32)
    return jnp.concatenate([values, rest, empty], axis=-2).astype(jnp.bfloat16)


def stage_kernel(
    place_ref,
    counts_ref,
    cols_ref,
    amps_hbm,
    own_ints_ref,
    left_ref,
    chunks_hbm,
    held_ref,
    total_ref,
    extra_ref,
    part_ref,
    in_sems,
    out_sems,
    extra_sem,
    part_sems,
):
    partners, chunk_count, chunk_rows, virtuals = amps_hbm.shape
    aux_count, slot_count, tile, _ = own_ints_ref.shape
    columns = virtuals // tile
    lines = aux_count * partners
    part = part_ref.shape[0] // (aux_count * slot_count)
    loads = [pltpu.make_async_copy(amps_hbm.at[index], held_ref.at[index], in_sems.at[index]) for index in range(partners)]

    def store(index, column):
        span = pl.ds(column * tile, tile)
        lines = pl.ds((index * columns + column) * chunk_rows, chunk_rows)
        return pltpu.make_async_copy(
            held_ref.at[index, :, :, span], chunks_hbm.at[:, lines, :], out_sems.at[index, column]
        )

    for load in loads:
        load.start()

    count = counts_ref[place_ref[0]]
    first = pl.multiple_of(place_ref[1] * part, part)
    for aux in range(aux_count):
        for slot in range(slot_count):
            live = (slot < count).astype(jnp.float32).astype(jnp.bfloat16)
            at = (aux * slot_count + slot) * part
            part_ref[at : at + part, :] = own_ints_ref[aux, slot, pl.ds(first, part), :] * live

    def send(chunk):
        lines = pl.ds(partners * tile + EXTRA, part_ref.shape[0])
        return pltpu.make_async_copy(part_ref, chunks_hbm.at[chunk, lines, :], part_sems.at[chunk])

    for chunk in range(chunk_count):
        send(chunk).start()

    for index in range(partners):
        loads[index].wait()
        for column in range(columns):
            store(index, column).start()
        for column in range(columns):
            rows = held_ref[index, :, :, column * tile : (column + 1) * tile].reshape(tile, tile)
            total = jnp.dot(left_ref[...], rows, preferred_element_type=jnp.float32)
            for aux in range(aux_count):
                line = aux * partners + index
                total_ref[column, line : line + 1, :] = total[aux : aux + 1]
    extra_ref[...] = pairs(total_ref[...], lines)
    extra = pltpu.make_async_copy(extra_ref, chunks_hbm.at[:, pl.ds(partners * tile, EXTRA), :], extra_sem)
    extra.start()
    for index in range(partners):
        for column in range(columns):
            store(index, column).wait()
    extra.wait()
    for chunk in range(chunk_count):
        send(chunk).wait()


def stage(place, counts, cols, amps, own_ints, left, parts):
    partners, chunk_count, chunk_rows, virtuals = amps.shape
    aux_count, slot_count, tile, _ = own_ints.shape
    columns = virtuals // tile
    part_rows = aux_count * slot_count * tile // parts
    return pl.pallas_call(
        stage_kernel,
        in_specs=[SMEM, SMEM, SMEM, HBM, VMEM, VMEM],
        out_specs=HBM,
        out_shape=jax.ShapeDtypeStruct((chunk_count, partners * tile + EXTRA + part_rows, tile), amps.dtype),
        scratch_shapes=[
            pltpu.VMEM(amps.shape, amps.dtype),
            pltpu.VMEM((columns, aux_count * partners, tile), jnp.float32),
            pltpu.VMEM((columns, EXTRA, tile), amps.dtype),
            pltpu.VMEM((part_rows, tile), amps.dtype),
            pltpu.SemaphoreType.DMA((partners,)),
            pltpu.SemaphoreType.DMA((partners, columns)),
            pltpu.SemaphoreType.DMA,
            pltpu.SemaphoreType.DMA((chunk_count,)),
        ],
        compiler_params=pltpu.CompilerParams(vmem_limit_bytes=60 * MIB),
        cost_estimate=pl.CostEstimate(flops=10**7, bytes_accessed=9 * MIB, transcendentals=0),
    )(place, counts, cols, amps, own_ints, left)


def pick_kernel(
    partners, lines, cols_ref, spread_hbm, first_hbm, later_hbm, ints_hbm, first_ref, held_ref, extra_ref, part_ref, in_sems, out_sems, extra_sems
):
    chunks, slots = in_sems.shape[1:]
    tile = held_ref.shape[3]
    part_rows = part_ref.shape[1]

    def fetch(partner, chunk, slot):
        source = spread_hbm.at[cols_ref[slot + 1, chunk], pl.ds(partner * tile, tile), :]
        place = first_ref.at[chunk] if partner == 0 else held_ref.at[partner - 1, chunk]
        return pltpu.make_async_copy(source, place.at[pl.ds(slot * tile, tile), :], in_sems.at[partner, chunk, slot])

    def store(partner, chunk):
        source = first_ref.at[chunk] if partner == 0 else held_ref.at[partner - 1, chunk]
        place = first_hbm.at[chunk] if partner == 0 else later_hbm.at[partner - 1, chunk]
        return pltpu.make_async_copy(source, place, out_sems.at[partner, chunk])

    extra = pltpu.make_async_copy(spread_hbm.at[:, pl.ds(partners * tile, EXTRA), :], extra_ref, extra_sems.at[0])
    part_in = pltpu.make_async_copy(spread_hbm.at[:, pl.ds(partners * tile + EXTRA, part_rows), :], part_ref, extra_sems.at[1])
    part_out = pltpu.make_async_copy(part_ref, ints_hbm, extra_sems.at[2])
    extra.start()
    for partner in range(partners):

        @pl.loop(0, chunks)
        def _(chunk, partner=partner):
            for slot in range(slots):
                fetch(partner, chunk, slot).start()

        if partner == 0:
            part_in.start()

    extra.wait()
    total = jnp.sum(extra_ref[...].astype(jnp.float32), axis=0)
    total = pairs(total[:lines] + total[lines : 2 * lines], lines)
    for chunk in range(chunks):
        first_ref[chunk, slots * tile :, :] = total

    for partner in range(partners):

        @pl.loop(0, chunks)
        def _(chunk, partner=partner):
            for slot in range(slots):
                fetch(partner, chunk, slot).wait()
            store(partner, chunk).start()

        if partner == 0:
            part_in.wait()
            part_out.start()

    for partner in range(partners):

        @pl.loop(0, chunks)
        def _(chunk, partner=partner):
            store(partner, chunk).wait()

    part_out.wait()


def pick(partners, lines, spread, cols):
    slots, chunks = cols.shape
    rows, tile = spread.shape[1:]
    shape = (partners - 1, chunks, (slots - 1) * tile, tile)
    first = (chunks, (slots - 1) * tile + EXTRA, tile)
    part_rows = rows - partners * tile - EXTRA
    return pl.pallas_call(
        functools.partial(pick_kernel, partners, lines),
        in_specs=[SMEM, HBM],
        out_specs=[HBM] * 3,
        out_shape=[
            jax.ShapeDtypeStruct(first, spread.dtype),
            jax.ShapeDtypeStruct(shape, spread.dtype),
            jax.ShapeDtypeStruct((chunks, part_rows, tile), spread.dtype),
        ],
        scratch_shapes=[
            pltpu.VMEM(first, spread.dtype),
            pltpu.VMEM(shape, spread.dtype),
            pltpu.VMEM((chunks, EXTRA, tile), spread.dtype),
            pltpu.VMEM((chunks, part_rows, tile), spread.dtype),
            pltpu.SemaphoreType.DMA((partners, chunks, slots - 1)),
            pltpu.SemaphoreType.DMA((partners, chunks)),
            pltpu.SemaphoreType.DMA((3,)),
        ],
        compiler_params=pltpu.CompilerParams(vmem_limit_bytes=60 * MIB),
        cost_estimate=pl.CostEstimate(flops=0, bytes_accessed=20 * MIB, transcendentals=0),
    )(cols, spread)


def ladder_kernel(
    partner, cols_ref, counts_ref, place_ref, amps_hbm, fetched_hbm, ints_hbm, cycle_ref, own_ints_ref, left_ref, *rest
):
    out_hbm, near_ref, far_ref, ints_ref, sums_ref, own_ref, half_ref, out_ref = rest[-12:-4]
    near_sems, far_sems, int_sems, out_sems = rest[-4:]
    tile_count, tile, _ = half_ref.shape
    aux_count, slot_count = own_ints_ref.shape[:2]
    partners, _, chunk_rows, virtuals = amps_hbm.shape
    wide = virtuals // ROW_CHUNKS
    part_rows = ints_ref.shape[1] // tile_count
    part = part_rows // (aux_count * slot_count)
    group = tile_count // INT_CHUNKS
    per_chunk = wide // tile

    def near_copy(chunk):
        span = pl.ds(pl.multiple_of(chunk * wide, wide), wide)
        return pltpu.make_async_copy(amps_hbm.at[partner, :, :, span], near_ref.at[:, :, span], near_sems.at[chunk])

    def far_copy(slot, chunk):
        lines = per_chunk * chunk_rows
        first = pl.multiple_of(slot * tile + chunk * lines, lines)
        return pltpu.make_async_copy(
            fetched_hbm.at[:, pl.ds(first, lines), :], far_ref.at[:, pl.ds(first, lines), :], far_sems.at[slot, chunk]
        )

    def int_copy(chunk):
        lines = group * part_rows
        span = pl.ds(pl.multiple_of(chunk * lines, lines), lines)
        return pltpu.make_async_copy(ints_hbm.at[:, span, :], ints_ref.at[:, span, :], int_sems.at[chunk])

    def out_copy(chunk):
        span = pl.ds(pl.multiple_of(chunk * group * tile, group * tile), group * tile)
        return pltpu.make_async_copy(out_ref.at[:, span], out_hbm.at[partner, :, span], out_sems.at[chunk])

    for chunk in range(ROW_CHUNKS):
        near_copy(chunk).start()
        for slot in range(slot_count - 1):
            far_copy(slot, chunk).start()
    for chunk in range(INT_CHUNKS):
        int_copy(chunk).start()

    count = counts_ref[place_ref[0]]
    for aux in range(aux_count):
        for slot in range(slot_count):
            live = (slot < count).astype(jnp.float32).astype(jnp.bfloat16)
            own_ref[aux * tile : (aux + 1) * tile, slot * tile : (slot + 1) * tile] = own_ints_ref[aux, slot] * live
    lines = aux_count * partners
    sums = jnp.sum(cycle_ref[...].astype(jnp.float32), axis=0)
    sums_ref[...] = sums[:, :lines] + sums[:, lines : 2 * lines]
    line = lax.broadcasted_iota(jnp.int32, (8, tile), 0)
    left = jnp.zeros((8, tile), jnp.float32)
    for aux in range(aux_count):
        left = jnp.where(line == aux, left_ref[aux : aux + 1, :].astype(jnp.float32), left)
    left = left.T

    @pl.loop(0, ROW_CHUNKS)
    def _(chunk):
        near_copy(chunk).wait()
        for slot in range(slot_count - 1):
            far_copy(slot, chunk).wait()
        for piece in range(per_chunk):
            column = chunk * per_chunk + piece
            span = pl.ds(pl.multiple_of(column * tile, tile), tile)
            rows = [near_ref[:, :, span].reshape(tile, tile)]
            for slot in range(slot_count - 1):
                first = pl.multiple_of(slot * tile + column * chunk_rows, chunk_rows)
                rows.append(far_ref[:, pl.ds(first, chunk_rows), :].reshape(tile, tile))
            total = jnp.dot(own_ref[...], jnp.concatenate(rows), preferred_element_type=jnp.float32).astype(jnp.bfloat16)
            for aux in range(aux_count):
                half_ref[column, :, aux * tile : (aux + 1) * tile] = total[aux * tile : (aux + 1) * tile]

    @pl.loop(0, INT_CHUNKS)
    def _(chunk):
        int_copy(chunk).wait()
        for piece in range(group):
            row = chunk * group + piece
            halves, ints = [], []
            for slot in range(slot_count):
                halves.append(half_ref[cols_ref[slot, row]])
                for aux in range(aux_count):
                    first = pl.multiple_of(row * part_rows + (aux * slot_count + slot) * part, part)
                    ints.append(ints_ref[:, pl.ds(first, part), :].reshape(tile, tile))
            total = lax.dot_general(
                jnp.concatenate(halves, axis=1),
                jnp.concatenate(ints, axis=1),
                (((1,), (1,)), ((), ())),
                preferred_element_type=jnp.float32,
            )
            for aux in range(aux_count):
                line = aux * partners + partner
                total += left[:, aux : aux + 1] * sums_ref[row, line : line + 1, :]
            out_ref[:, pl.ds(pl.multiple_of(row * tile, tile), tile)] = total.astype(jnp.bfloat16)
        out_copy(chunk).start()

    @pl.loop(0, INT_CHUNKS)
    def _(chunk):
        out_copy(chunk).wait()


def ladder(partner, cols, counts, place, amps, fetched, ints, cycle, own_ints, left, before):
    partners, chunks, chunk_rows, virtuals = amps.shape
    aux_count, slot_count, tile, _ = own_ints.shape
    tile_count = virtuals // tile
    args = [cols, counts, place, amps, fetched, ints, cycle, own_ints, left]
    specs = [SMEM] * 3 + [HBM] * 3 + [VMEM] * 3
    aliases = {}
    if before is not None:
        aliases = {len(args): 0}
        args.append(before)
        specs.append(HBM)
    return pl.pallas_call(
        functools.partial(ladder_kernel, partner),
        in_specs=specs,
        out_specs=HBM,
        out_shape=jax.ShapeDtypeStruct((partners, tile, virtuals), jnp.bfloat16),
        input_output_aliases=aliases,
        scratch_shapes=[
            pltpu.VMEM((chunks, chunk_rows, virtuals), jnp.bfloat16),
            pltpu.VMEM((chunks, (slot_count - 1) * tile, tile), jnp.bfloat16),
            pltpu.VMEM(ints.shape, jnp.bfloat16),
            pltpu.VMEM((tile_count, aux_count * partners, tile), jnp.float32),
            pltpu.VMEM((aux_count * tile, slot_count * tile), jnp.bfloat16),
            pltpu.VMEM((tile_count, tile, aux_count * tile), jnp.bfloat16),
            pltpu.VMEM((tile, virtuals), jnp.bfloat16),
            pltpu.SemaphoreType.DMA((ROW_CHUNKS,)),
            pltpu.SemaphoreType.DMA((slot_count - 1, ROW_CHUNKS)),
            pltpu.SemaphoreType.DMA((INT_CHUNKS,)),
            pltpu.SemaphoreType.DMA((INT_CHUNKS,)),
        ],
        compiler_params=pltpu.CompilerParams(vmem_limit_bytes=60 * MIB),
        cost_estimate=pl.CostEstimate(flops=6 * 10**9, bytes_accessed=20 * MIB, transcendentals=0),
    )(*args)


def cut_kernel(first, source_hbm, after_hbm, out_ref, sem):
    copy = pltpu.make_async_copy(source_hbm.at[:, pl.ds(first, out_ref.shape[1]), :], out_ref, sem)
    copy.start()
    copy.wait()


def cut(source, first, rows, after):
    chunks, _, width = source.shape
    return pl.pallas_call(
        functools.partial(cut_kernel, first),
        in_specs=[HBM, HBM],
        out_specs=VMEM,
        out_shape=jax.ShapeDtypeStruct((chunks, rows, width), source.dtype),
        scratch_shapes=[pltpu.SemaphoreType.DMA],
        compiler_params=pltpu.CompilerParams(vmem_limit_bytes=60 * MIB),
        cost_estimate=pl.CostEstimate(flops=0, bytes_accessed=2 * MIB, transcendentals=0),
    )(source, after)


def body(amplitudes, ladder_ints, tile_cols, tile_counts, cycle_ints):
    tile_count, slot_count = tile_cols.shape
    aux_count = ladder_ints.shape[0]
    tile = ladder_ints.shape[3]
    partners = amplitudes.shape[1]
    virtuals = amplitudes.shape[3]
    parts = lax.axis_size("occ")
    chunked = amplitudes[0].reshape(partners, tile_count, tile // tile_count, virtuals)
    own_ints = ladder_ints[:, 0]
    left = cycle_ints[:, 0, :]
    place = jnp.stack([lax.axis_index("vir"), lax.axis_index("occ")])
    lines = aux_count * partners
    cols = tile_cols.T

    chunks = stage(place, tile_counts, cols, chunked, own_ints, left, parts)
    spread = lax.all_to_all(chunks, "vir", split_axis=0, concat_axis=0, tiled=True)
    first, later, here = pick(partners, lines, spread, cols)
    picked = [first] + [later[index] for index in range(partners - 1)]

    ints = lax.all_gather(here, "occ", axis=0).reshape(parts, -1, tile)

    out = None
    for partner in range(partners):
        fetched = lax.all_to_all(picked[partner], "vir", split_axis=0, concat_axis=0, tiled=True)
        if partner == 0:
            sums = cut(fetched, (slot_count - 1) * tile, EXTRA, ints)
            cycle = lax.all_gather(sums, "occ", axis=0)
        out = ladder(partner, cols, tile_counts, place, chunked, fetched, ints, cycle, own_ints, left, out)
    return out[None]


def solution(mesh):
    in_specs = (
        P("occ", None, "vir", None),
        P(None, "vir", None, None, None),
        P(),
        P(),
        P(None, "occ", "vir"),
    )
    out_specs = P("occ", None, "vir", None)
    return jax.shard_map(body, mesh=mesh, in_specs=in_specs, out_specs=out_specs, check_vma=False)
```

time: 498 us -> 239 us (0.48)
  local copies, waits for them, and re-layouts: 106 us -> 0 us
  matrix products: 79.4 us -> 0 us
  waiting for transfers between devices: 95.5 us -> 39.6 us
  Pallas kernels: 0 us -> 46.4 us
  blocking collectives: 178 us -> 134 us
  other arithmetic: 10.9 us -> 0.65 us
  starting transfers between devices: 12.8 us -> 4.58 us
    psum x1 -> x0, blocking collectives: 178 us -> none  [body(): cycle_total = lax.psum(cycle_local, ('occ', 'vir'))]
    all_to_all x0 -> x2, blocking collectives: none -> 134 us  [the longest x1 77.2 us: body(): lax.all_to_all(chunks, 'vir', split_axis=0, concat_axis=0, tiled=True)]
    dot_general x8 -> x0, matrix products: 79.4 us -> none  [the longest x3 39.3 us: body(): jnp.einsum('qaxc,jacd->qjaxd', int_tiles[:, :, slot_index], chosen, prefe...]
    all_to_all x2 -> x1, waiting for transfers between devices: 73.6 us -> 11.9 us  [body(): lax.all_to_all(picked[partner], 'vir', split_axis=0, concat_axis=0, tiled...]
    pallas_call x0 -> x5, Pallas kernels: none -> 46.4 us  [the longest x2 29.9 us: ladder(): pl.pallas_call(functools.partial(ladder_kernel, partner), in_specs=specs,...]
    gather x6 -> x0, local copies, waits for them, and re-layouts: 39.5 us -> none  [the longest x3 24.4 us: ladder_from(): picked = jnp.take(blocks, tile_cols[:, slot_index], axis=3)]
    all_to_all x2 -> x0, local copies, waits for them, and re-layouts: 18.8 us -> none  [the longest x1 11.1 us: body(): lax.all_to_all(amplitudes, 'vir', split_axis=3, concat_axis=2, tiled=True)]
    reshape x1 -> x0, local copies, waits for them, and re-layouts: 16.4 us -> none  [body(): total.astype(jnp.bfloat16)]
  transfers between devices with their start and end apart: 3 -> 3, of which waited for: 2 -> 3; matrix products, arithmetic and copies ran while one was open for 8% -> 0% of each run, Pallas kernels for 0% -> 7%
where the time goes in v2:
time: 239 us
  blocking collectives  134 us (56%)
  Pallas kernels  46.4 us (19%)
  waiting for transfers between devices  39.6 us (17%)
  between operations  13.5 us (6%)
  starting transfers between devices  4.58 us (2%)
    all_to_all x1, blocking collectives, body(): lax.all_to_all(chunks, 'vir', split_axis=0, concat_axis=0, tiled=True)  77.2 us
    all_to_all x1, blocking collectives, body(): lax.all_to_all(picked[partner], 'vir', split_axis=0, concat_axis=0, tiled...  57 us
    pallas_call x2, Pallas kernels, ladder(): pl.pallas_call(functools.partial(ladder_kernel, partner), in_specs=specs,...  29.9 us
    all_gather x1, waiting for transfers between devices, body(): cycle = lax.all_gather(sums, 'occ', axis=0)  23.9 us
    all_to_all x1, waiting for transfers between devices, body(): lax.all_to_all(picked[partner], 'vir', split_axis=0, concat_axis=0, tiled...  11.9 us
    pallas_call x1, Pallas kernels, pick(): pl.pallas_call(functools.partial(pick_kernel, partners, lines), in_specs=...  9.08 us
    pallas_call x1, Pallas kernels, stage(): pl.pallas_call(stage_kernel, in_specs=[SMEM, SMEM, SMEM, HBM, VMEM, VMEM]...  5.88 us
  transfers between devices with their start and end apart: 3, of which 3 were waited for; matrix products, arithmetic and copies ran while one was open for 0% of the time, Pallas kernels for 7%

profile of v2, /device:TPU:0, one launch (start us, length us, event | category | flops | bytes accessed | tf_op | source)
XLA Modules:
  0.0 238.8 jit_solution(11883448542784628355)
XLA Ops:
  6.5 0.0 all-gather.5.cloned.1.call-start
  6.5 0.7 pad_add_fusion.place_ref
  7.2 5.9 %shard_map.55 = bf16[16,720,256]{2,1,0:T(8,128)(2,1)} custom-call(s32[2]{0:T(128)} %pad_add_fusion.place_ref, s32[16]{0:T(128)} %counts_ref.5, s32[3,16]{1,0:T(4,128)} %bitcast.22, bf16[2,16,16,4096]{3,2,1,0:T(8,128)(2,1)} %bitcast.13, bf16[2,3,256,256]{3,2,1,0:T(8,128)(2,1)} %bitcast.16, bf16[2,256]{1,0:T(2,128)(2,1)} %bitcast.26), custom_call_target="tpu_custom_call" | custom-call | flops 10000000 | bytes 9437184 | tf_op jit(solution)/shard_map/pallas_call | solution.py:101
  13.1 77.2 %all_to_all.15.spread_hbm = bf16[16,720,256]{2,1,0:T(8,128)(2,1)} all-to-all(bf16[16,720,256]{2,1,0:T(8,128)(2,1)} %shard_map.55), channel_id=1, replica_groups=mesh['occ'=8,'vir'=16] {'vir'}, dimensions={0} | all-to-all | bytes 11796480 | tf_op jit(solution)/shard_map/all_to_all | solution.py:376
  90.3 9.1 %shard_map.56 = (bf16[16,528,256]{2,1,0:T(8,128)(2,1)}, bf16[1,16,512,256]{3,2,1,0:T(8,128)(2,1)}, bf16[16,192,256]{2,1,0:T(8,128)(2,1)}) custom-call(s32[3,16]{1,0:T(4,128)} %bitcast.23, bf16[16,720,256]{2,1,0:T(8,128)(2,1)} %all_to_all.15.spread_hbm), custom_call_target="tpu_custom_call" | custom-call | bytes 20971520 | tf_op jit(solution)/shard_map/pallas_call | solution.py:185
  99.4 0.0 all-gather.5.cloned.1.call-update
  99.4 57.0 %all_to_all.16.source_hbm.fetched_hbm = bf16[16,528,256]{2,1,0:T(8,128)(2,1)} all-to-all(bf16[16,528,256]{2,1,0:T(8,128)(2,1)} %get-tuple-element.10), channel_id=1, replica_groups=mesh['occ'=8,'vir'=16] {'vir'}, dimensions={0} | all-to-all | bytes 8650752 | tf_op jit(solution)/shard_map/all_to_all | solution.py:384
  156.3 4.5 %all-to-all-start.1 = ((bf16[16,512,256]{2,1,0:T(8,128)(2,1)}), bf16[16,512,256]{2,1,0:T(8,128)(2,1)}, u32[]{:S(2)}, u32[]{:S(2)}) async-start(bf16[16,512,256]{2,1,0:T(8,128)(2,1)} %bitcast.21), calls=%async_computation.1 | async-start | bytes 8388608 | tf_op jit(solution)/shard_map/all_to_all | solution.py:384
  160.9 0.0 all-gather.7.cloned.1.call-start
  160.9 3.7 %all-gather.5.cloned.1.call-done = bf16[128,192,256]{2,1,0:T(8,128)(2,1)} async-done(((bf16[16,192,256]{2,1,0:T(8,128)(2,1)}), bf16[128,192,256]{2,1,0:T(8,128)(2,1)}) %all-gather.5.cloned.1.call-update) | async-done | bytes 12582928 | tf_op jit(solution)/shard_map/all_gather | solution.py:380
  164.7 1.6 shard_map.57
  166.2 0.0 all-gather.7.cloned.1.call-update
  166.3 23.9 %all-gather.7.cloned.1.call-done = bf16[128,16,256]{2,1,0:T(8,128)(2,1)} async-done(((bf16[16,16,256]{2,1,0:T(8,128)(2,1)}), bf16[128,16,256]{2,1,0:T(8,128)(2,1)}) %all-gather.7.cloned.1.call-update) | async-done | bytes 1048592 | tf_op jit(solution)/shard_map/all_gather | solution.py:387
  190.2 14.9 %shard_map.58.rest_0_ = bf16[2,256,4096]{2,1,0:T(8,128)(2,1)} custom-call(s32[3,16]{1,0:T(4,128)} %bitcast.24, s32[16]{0:T(128)} %counts_ref.5, s32[2]{0:T(128)} %pad_add_fusion.place_ref, bf16[2,16,16,4096]{3,2,1,0:T(8,128)(2,1)} %bitcast.14, bf16[16,528,256]{2,1,0:T(8,128)(2,1)} %all_to_all.16.source_hbm.fetched_hbm, bf16[8,3072,256]{2,1,0:T(8,128)(2,1)} %bitcast.11, ...), custom_call_target="tpu_custom_call" | custom-call | flops 6000000000 | bytes 20971520 | tf_op jit(solution)/shard_map/pallas_call | solution.py:318
  205.1 11.9 %all-to-all-done.1.fetched_hbm = bf16[16,512,256]{2,1,0:T(8,128)(2,1)} async-done(((bf16[16,512,256]{2,1,0:T(8,128)(2,1)}), bf16[16,512,256]{2,1,0:T(8,128)(2,1)}, u32[]{:S(2)}, u32[]{:S(2)}) %all-to-all-start.1) | async-done | bytes 4194336 | tf_op jit(solution)/shard_map/all_to_all | solution.py:384
  217.0 14.9 %shard_map.59 = bf16[2,256,4096]{2,1,0:T(8,128)(2,1)} custom-call(s32[3,16]{1,0:T(4,128)} %bitcast.25, s32[16]{0:T(128)} %counts_ref.5, s32[2]{0:T(128)} %pad_add_fusion.place_ref, bf16[2,16,16,4096]{3,2,1,0:T(8,128)(2,1)} %bitcast.15, bf16[16,512,256]{2,1,0:T(8,128)(2,1)} %all-to-all-done.1.fetched_hbm, ...), custom_call_target="tpu_custom_call", output_to_operand_aliasing={{}: (9, {})} | custom-call | flops 6000000000 | bytes 20971520 | tf_op jit(solution)/shard_map/pallas_call | solution.py:318
Async XLA Ops:
  6.5 158.1 %all-gather.5.cloned.1.call-start = ((), (), s32[]{:S(2)}) async-start(), calls=%async_computation.3 | async-start | bytes 14155776 | tf_op jit(solution)/shard_map/all_gather | solution.py:380
  156.3 60.7 %all-to-all-start.1 = ((bf16[16,512,256]{2,1,0:T(8,128)(2,1)}), bf16[16,512,256]{2,1,0:T(8,128)(2,1)}, u32[]{:S(2)}, u32[]{:S(2)}) async-start(bf16[16,512,256]{2,1,0:T(8,128)(2,1)} %bitcast.21), calls=%async_computation.1 | async-start | bytes 8388608 | tf_op jit(solution)/shard_map/all_to_all | solution.py:384
  160.9 29.3 %all-gather.7.cloned.1.call-start = ((), (), s32[]{:S(2)}) async-start(), calls=%async_computation.4 | async-start | bytes 1179648 | tf_op jit(solution)/shard_map/all_gather | solution.py:387
Sparse Core Ops, SparseCore 0:
  99.5 65.1 all-gather.4
  166.4 23.7 all-gather.6

commit v3 on v0

v3 whole, which is shorter than its diff:
```python
import functools

import jax
import jax.numpy as jnp
from jax import lax
from jax.experimental import pallas as pl
from jax.experimental.pallas import tpu as pltpu
from jax.sharding import PartitionSpec as P

ROW_CHUNKS = 4
INT_CHUNKS = 4
MIB = 2**20
HBM = pl.BlockSpec(memory_space=pltpu.HBM)
VMEM = pl.BlockSpec(memory_space=pltpu.VMEM)
SMEM = pl.BlockSpec(memory_space=pltpu.SMEM)


def stage_kernel(
    place_ref, counts_ref, cols_ref, amps_hbm, own_ints_ref, left_ref, chunks_hbm, held_ref, total_ref, same_ref, in_sems, out_sems, same_sems
):
    partners, chunk_count, chunk_rows, virtuals = amps_hbm.shape
    aux_count, slot_count, tile, _ = own_ints_ref.shape
    columns = virtuals // tile
    lines = total_ref.shape[0]
    part = (same_ref.shape[0] - lines) // (aux_count * slot_count)

    def load(index):
        return pltpu.make_async_copy(amps_hbm.at[index], held_ref.at[index], in_sems.at[index])

    def store(index, column):
        place = pl.ds((index * columns + column) * chunk_rows, chunk_rows)
        source = held_ref.at[index, :, :, pl.ds(column * tile, tile)]
        return pltpu.make_async_copy(source, chunks_hbm.at[:, place, :], out_sems.at[index, column])

    def send(chunk):
        place = pl.ds(partners * tile, same_ref.shape[0])
        return pltpu.make_async_copy(same_ref, chunks_hbm.at[chunk, place, :], same_sems.at[chunk])

    for index in range(partners):
        load(index).start()

    count = counts_ref[place_ref[0]]
    first = pl.multiple_of(place_ref[1] * part, part)
    for aux in range(aux_count):
        for slot in range(slot_count):
            live = (slot < count).astype(jnp.float32).astype(jnp.bfloat16)
            at = lines + (aux * slot_count + slot) * part
            same_ref[at : at + part, :] = own_ints_ref[aux, slot, pl.ds(first, part), :] * live

    for index in range(partners):
        load(index).wait()
        for column in range(columns):
            store(index, column).start()
        for column in range(columns):
            rows = held_ref[index, :, :, column * tile : (column + 1) * tile].reshape(tile, tile)
            total = jnp.dot(left_ref[...], rows, preferred_element_type=jnp.float32)
            for aux in range(aux_count):
                line = (aux * partners + index) * columns + column
                total_ref[line : line + 1, :] = total[aux : aux + 1]
    same_ref[:lines, :] = total_ref[...].astype(jnp.bfloat16)
    for chunk in range(chunk_count):
        send(chunk).start()
    for index in range(partners):
        for column in range(columns):
            store(index, column).wait()
    for chunk in range(chunk_count):
        send(chunk).wait()


def stage(place, counts, cols, amps, own_ints, left, parts):
    partners, chunk_count, chunk_rows, virtuals = amps.shape
    aux_count, slot_count, tile, _ = own_ints.shape
    columns = virtuals // tile
    lines = aux_count * partners * columns
    same = lines + aux_count * slot_count * tile // parts
    return pl.pallas_call(
        stage_kernel,
        in_specs=[SMEM, SMEM, SMEM, HBM, VMEM, VMEM],
        out_specs=HBM,
        out_shape=jax.ShapeDtypeStruct((chunk_count, partners * tile + same, tile), amps.dtype),
        scratch_shapes=[
            pltpu.VMEM(amps.shape, amps.dtype),
            pltpu.VMEM((lines, tile), jnp.float32),
            pltpu.VMEM((same, tile), amps.dtype),
            pltpu.SemaphoreType.DMA((partners,)),
            pltpu.SemaphoreType.DMA((partners, columns)),
            pltpu.SemaphoreType.DMA((chunk_count,)),
        ],
        compiler_params=pltpu.CompilerParams(vmem_limit_bytes=60 * MIB),
        cost_estimate=pl.CostEstimate(flops=10**7, bytes_accessed=10 * MIB, transcendentals=0),
    )(place, counts, cols, amps, own_ints, left)


def pick_kernel(partners, cols_ref, spread_hbm, out_hbm, shared_hbm, held_ref, sums_ref, shared_ref, in_sems, out_sems, part_sems, sems):
    chunks, slots = in_sems.shape
    lines = sums_ref.shape[1]
    rows = held_ref.shape[1] // slots
    part = spread_hbm.shape[1] - rows - lines

    def fetch(chunk, slot):
        source = spread_hbm.at[cols_ref[slot + 1, chunk], pl.ds(0, rows), :]
        return pltpu.make_async_copy(source, held_ref.at[chunk, pl.ds(slot * rows, rows), :], in_sems.at[chunk, slot])

    def store(chunk):
        return pltpu.make_async_copy(held_ref.at[chunk], out_hbm.at[chunk], out_sems.at[chunk])

    def part_copy(chunk):
        source = spread_hbm.at[chunk, pl.ds(rows + lines, part), :]
        return pltpu.make_async_copy(source, shared_ref.at[pl.ds(chunk * part, part), :], part_sems.at[chunk])

    sums_in = pltpu.make_async_copy(spread_hbm.at[:, pl.ds(rows, lines), :], sums_ref, sems.at[0])
    shared_out = pltpu.make_async_copy(shared_ref, shared_hbm, sems.at[1])
    sums_in.start()
    for chunk in range(chunks):
        part_copy(chunk).start()

    @pl.loop(0, chunks)
    def _(chunk):
        for slot in range(slots):
            fetch(chunk, slot).start()

    sums_in.wait()
    total = jnp.sum(sums_ref[...].astype(jnp.float32), axis=0)
    value = total.astype(jnp.bfloat16)
    shared_ref[chunks * part : chunks * part + lines, :] = value
    shared_ref[chunks * part + lines :, :] = (total - value.astype(jnp.float32)).astype(jnp.bfloat16)
    for chunk in range(chunks):
        part_copy(chunk).wait()
    shared_out.start()

    @pl.loop(0, chunks)
    def _(chunk):
        for slot in range(slots):
            fetch(chunk, slot).wait()
        store(chunk).start()

    @pl.loop(0, chunks)
    def _(chunk):
        store(chunk).wait()

    shared_out.wait()


def pick(partners, lines, spread, cols):
    slots, chunks = cols.shape
    rows, tile = spread.shape[1:]
    part = rows - partners * tile - lines
    shape = (chunks, (slots - 1) * partners * tile, tile)
    shared = (chunks * part + 2 * lines, tile)
    return pl.pallas_call(
        functools.partial(pick_kernel, partners),
        in_specs=[SMEM, HBM],
        out_specs=[HBM, HBM],
        out_shape=[jax.ShapeDtypeStruct(shape, spread.dtype), jax.ShapeDtypeStruct(shared, spread.dtype)],
        scratch_shapes=[
            pltpu.VMEM(shape, spread.dtype),
            pltpu.VMEM((chunks, lines, tile), spread.dtype),
            pltpu.VMEM(shared, spread.dtype),
            pltpu.SemaphoreType.DMA((chunks, slots - 1)),
            pltpu.SemaphoreType.DMA((chunks,)),
            pltpu.SemaphoreType.DMA((chunks,)),
            pltpu.SemaphoreType.DMA((2,)),
        ],
        compiler_params=pltpu.CompilerParams(vmem_limit_bytes=60 * MIB),
        cost_estimate=pl.CostEstimate(flops=0, bytes_accessed=20 * MIB, transcendentals=0),
    )(cols, spread)


def ladder_kernel(cols_ref, counts_ref, place_ref, amps_hbm, fetched_hbm, ints_hbm, own_ints_ref, left_ref, out_hbm, *rest):
    near_ref, far_ref, ints_ref, cycle_ref, sums_ref, own_ref, half_ref, out_ref = rest[:8]
    near_sems, far_sems, int_sems, cycle_sem, out_sems = rest[8:]
    aux_count, slot_count, tile, _ = own_ints_ref.shape
    partners, _, chunk_rows, virtuals = amps_hbm.shape
    tile_count = virtuals // tile
    held = ints_ref.shape[1]
    part_rows = held // tile_count
    part = part_rows // (aux_count * slot_count)
    wide = virtuals // ROW_CHUNKS
    per_chunk = wide // tile
    group = tile_count // INT_CHUNKS
    lines = sums_ref.shape[0]

    def near_copy(partner, chunk):
        span = pl.ds(pl.multiple_of(chunk * wide, wide), wide)
        source = amps_hbm.at[partner, :, :, span]
        return pltpu.make_async_copy(source, near_ref.at[partner, :, :, span], near_sems.at[partner, chunk])

    def far_copy(partner, slot, chunk):
        rows = per_chunk * chunk_rows
        span = pl.ds(pl.multiple_of((slot * partners + partner) * tile + chunk * rows, rows), rows)
        return pltpu.make_async_copy(fetched_hbm.at[:, span, :], far_ref.at[:, span, :], far_sems.at[partner, slot, chunk])

    def int_copy(chunk):
        rows = group * part_rows
        span = pl.ds(pl.multiple_of(chunk * rows, rows), rows)
        return pltpu.make_async_copy(ints_hbm.at[:, span, :], ints_ref.at[:, span, :], int_sems.at[chunk])

    def out_copy(chunk):
        span = pl.ds(pl.multiple_of(chunk * group * tile, group * tile), group * tile)
        return pltpu.make_async_copy(out_ref.at[:, span], out_hbm.at[:, span], out_sems.at[chunk])

    cycle_copy = pltpu.make_async_copy(ints_hbm.at[:, pl.ds(held, 2 * lines), :], cycle_ref, cycle_sem)

    for chunk in range(ROW_CHUNKS):
        for partner in range(partners):
            near_copy(partner, chunk).start()
            for slot in range(slot_count - 1):
                far_copy(partner, slot, chunk).start()
    cycle_copy.start()
    for chunk in range(INT_CHUNKS):
        int_copy(chunk).start()

    count = counts_ref[place_ref[0]]
    for aux in range(aux_count):
        for slot in range(slot_count):
            live = (slot < count).astype(jnp.float32).astype(jnp.bfloat16)
            own_ref[aux * tile : (aux + 1) * tile, slot * tile : (slot + 1) * tile] = own_ints_ref[aux, slot] * live
    line = lax.broadcasted_iota(jnp.int32, (8, tile), 0)
    left = jnp.zeros((8, tile), jnp.float32)
    for aux in range(aux_count):
        left = jnp.where(line == aux, left_ref[aux : aux + 1, :].astype(jnp.float32), left)
    left = left.T

    @pl.loop(0, ROW_CHUNKS)
    def _(chunk):
        for partner in range(partners):
            near_copy(partner, chunk).wait()
            for slot in range(slot_count - 1):
                far_copy(partner, slot, chunk).wait()
        for piece in range(per_chunk):
            column = chunk * per_chunk + piece
            span = pl.ds(pl.multiple_of(column * tile, tile), tile)
            for partner in range(partners):
                rows = [near_ref[partner, :, :, span].reshape(tile, tile)]
                for slot in range(slot_count - 1):
                    first = pl.multiple_of((slot * partners + partner) * tile + column * chunk_rows, chunk_rows)
                    rows.append(far_ref[:, pl.ds(first, chunk_rows), :].reshape(tile, tile))
                total = jnp.dot(own_ref[...], jnp.concatenate(rows), preferred_element_type=jnp.float32).astype(jnp.bfloat16)
                for aux in range(aux_count):
                    half_ref[column, partner * tile : (partner + 1) * tile, aux * tile : (aux + 1) * tile] = total[
                        aux * tile : (aux + 1) * tile
                    ]

    cycle_copy.wait()
    sums = jnp.sum(cycle_ref[...].astype(jnp.float32), axis=0)
    sums_ref[...] = sums[:lines] + sums[lines:]

    @pl.loop(0, INT_CHUNKS)
    def _(chunk):
        int_copy(chunk).wait()
        for piece in range(group):
            row = chunk * group + piece
            halves, ints = [], []
            for slot in range(slot_count):
                halves.append(half_ref[cols_ref[slot, row]])
                for aux in range(aux_count):
                    first = pl.multiple_of(row * part_rows + (aux * slot_count + slot) * part, part)
                    ints.append(ints_ref[:, pl.ds(first, part), :].reshape(tile, tile))
            total = lax.dot_general(
                jnp.concatenate(halves, axis=1),
                jnp.concatenate(ints, axis=1),
                (((1,), (1,)), ((), ())),
                preferred_element_type=jnp.float32,
            )
            span = pl.ds(pl.multiple_of(row * tile, tile), tile)
            for partner in range(partners):
                part_total = total[partner * tile : (partner + 1) * tile]
                for aux in range(aux_count):
                    right = sums_ref[pl.ds((aux * partners + partner) * tile_count + row, 1), :]
                    part_total += left[:, aux : aux + 1] * right
                out_ref[partner * tile : (partner + 1) * tile, span] = part_total.astype(jnp.bfloat16)
        out_copy(chunk).start()

    @pl.loop(0, INT_CHUNKS)
    def _(chunk):
        out_copy(chunk).wait()


def ladder(cols, counts, place, amps, fetched, ints, own_ints, left):
    partners, chunks, chunk_rows, virtuals = amps.shape
    aux_count, slot_count, tile, _ = own_ints.shape
    parts = ints.shape[0]
    tile_count = virtuals // tile
    lines = aux_count * partners * tile_count
    held = ints.shape[1] - 2 * lines
    return pl.pallas_call(
        ladder_kernel,
        in_specs=[SMEM] * 3 + [HBM] * 3 + [VMEM] * 2,
        out_specs=HBM,
        out_shape=jax.ShapeDtypeStruct((partners * tile, virtuals), jnp.bfloat16),
        scratch_shapes=[
            pltpu.VMEM(amps.shape, jnp.bfloat16),
            pltpu.VMEM(fetched.shape, jnp.bfloat16),
            pltpu.VMEM((parts, held, tile), jnp.bfloat16),
            pltpu.VMEM((parts, 2 * lines, tile), jnp.bfloat16),
            pltpu.VMEM((lines, tile), jnp.float32),
            pltpu.VMEM((aux_count * tile, slot_count * tile), jnp.bfloat16),
            pltpu.VMEM((tile_count, partners * tile, aux_count * tile), jnp.bfloat16),
            pltpu.VMEM((partners * tile, virtuals), jnp.bfloat16),
            pltpu.SemaphoreType.DMA((partners, ROW_CHUNKS)),
            pltpu.SemaphoreType.DMA((partners, slot_count - 1, ROW_CHUNKS)),
            pltpu.SemaphoreType.DMA((INT_CHUNKS,)),
            pltpu.SemaphoreType.DMA,
            pltpu.SemaphoreType.DMA((INT_CHUNKS,)),
        ],
        compiler_params=pltpu.CompilerParams(vmem_limit_bytes=60 * MIB),
        cost_estimate=pl.CostEstimate(flops=12 * 10**9, bytes_accessed=30 * MIB, transcendentals=0),
    )(cols, counts, place, amps, fetched, ints, own_ints, left)


def body(amplitudes, ladder_ints, tile_cols, tile_counts, cycle_ints):
    tile_count, slot_count = tile_cols.shape
    aux_count = ladder_ints.shape[0]
    tile = ladder_ints.shape[3]
    partners = amplitudes.shape[1]
    virtuals = amplitudes.shape[3]
    parts = lax.axis_size("occ")
    amps = amplitudes[0].reshape(partners, tile_count, tile // tile_count, virtuals)
    own_ints = ladder_ints[:, 0]
    left = cycle_ints[:, 0, :]
    place = jnp.stack([lax.axis_index("vir"), lax.axis_index("occ")])
    cols = tile_cols.T
    lines = aux_count * partners * tile_count

    chunks = stage(place, tile_counts, cols, amps, own_ints, left, parts)
    spread = lax.all_to_all(chunks, "vir", split_axis=0, concat_axis=0, tiled=True)
    picked, shared = pick(partners, lines, spread, cols)
    ints = lax.all_gather(shared, "occ", axis=0)
    fetched = lax.all_to_all(picked, "vir", split_axis=0, concat_axis=0, tiled=True)
    out = ladder(cols, tile_counts, place, amps, fetched, ints, own_ints, left)
    return out.reshape(1, partners, tile, virtuals)


def solution(mesh):
    in_specs = (
        P("occ", None, "vir", None),
        P(None, "vir", None, None, None),
        P(),
        P(),
        P(None, "occ", "vir"),
    )
    out_specs = P("occ", None, "vir", None)
    return jax.shard_map(body, mesh=mesh, in_specs=in_specs, out_specs=out_specs, check_vma=False)
```

time: 498 us -> 231 us (0.46)
  local copies, waits for them, and re-layouts: 106 us -> 0 us
  waiting for transfers between devices: 95.5 us -> 0.02 us
  matrix products: 79.4 us -> 0 us
  Pallas kernels: 0 us -> 35 us
  starting transfers between devices: 12.8 us -> 0.01 us
  other arithmetic: 10.9 us -> 0.64 us
    all_to_all x0 -> x2, blocking collectives: none -> 182 us  [the longest x1 101 us: body(): lax.all_to_all(picked, 'vir', split_axis=0, concat_axis=0, tiled=True)]
    psum x1 -> x0, blocking collectives: 178 us -> none  [body(): cycle_total = lax.psum(cycle_local, ('occ', 'vir'))]
    dot_general x8 -> x0, matrix products: 79.4 us -> none  [the longest x3 39.3 us: body(): jnp.einsum('qaxc,jacd->qjaxd', int_tiles[:, :, slot_index], chosen, prefe...]
    all_to_all x2 -> x0, waiting for transfers between devices: 73.6 us -> none  [the longest x1 73.6 us: body(): lax.all_to_all(amplitudes, 'vir', split_axis=3, concat_axis=2, tiled=True)]
    gather x6 -> x0, local copies, waits for them, and re-layouts: 39.5 us -> none  [the longest x3 24.4 us: ladder_from(): picked = jnp.take(blocks, tile_cols[:, slot_index], axis=3)]
    pallas_call x0 -> x3, Pallas kernels: none -> 35 us  [the longest x1 20.2 us: ladder(): pl.pallas_call(ladder_kernel, in_specs=[SMEM] * 3 + [HBM] * 3 + [VMEM] *...]
    all_gather x1, waiting for transfers between devices: 21.9 us -> 0.01 us  [body(): ints = lax.all_gather(shared, 'occ', axis=0)]
    all_to_all x2 -> x0, local copies, waits for them, and re-layouts: 18.8 us -> none  [the longest x1 11.1 us: body(): lax.all_to_all(amplitudes, 'vir', split_axis=3, concat_axis=2, tiled=True)]
  transfers between devices with their start and end apart: 3 -> 1, of which waited for: 2 -> 0; matrix products, arithmetic and copies ran while one was open for 8% -> 0% of each run, Pallas kernels for 0% -> 0%
where the time goes in v3:
time: 231 us
  blocking collectives  182 us (79%)
  Pallas kernels  35 us (15%)
  between operations  13.4 us (6%)
    all_to_all x1, blocking collectives, body(): lax.all_to_all(picked, 'vir', split_axis=0, concat_axis=0, tiled=True)  101 us
    all_to_all x1, blocking collectives, body(): lax.all_to_all(chunks, 'vir', split_axis=0, concat_axis=0, tiled=True)  81.4 us
    pallas_call x1, Pallas kernels, ladder(): pl.pallas_call(ladder_kernel, in_specs=[SMEM] * 3 + [HBM] * 3 + [VMEM] *...  20.2 us
    pallas_call x1, Pallas kernels, pick(): pl.pallas_call(functools.partial(pick_kernel, partners), in_specs=[SMEM,...  8.94 us
    pallas_call x1, Pallas kernels, stage(): pl.pallas_call(stage_kernel, in_specs=[SMEM, SMEM, SMEM, HBM, VMEM, VMEM]...  5.87 us
  transfers between devices with their start and end apart: 1, of which 0 were waited for; matrix products, arithmetic and copies ran while one was open for 0% of the time, Pallas kernels for 0%

profile of v3, /device:TPU:0, one launch (start us, length us, event | category | flops | bytes accessed | tf_op | source)
XLA Modules:
  0.0 231.1 jit_solution(8198981728431091835)
XLA Ops:
  6.5 0.0 all-gather.3.cloned.1.call-start
  6.5 0.6 pad_add_fusion.place_ref
  7.2 5.9 %shard_map.55 = bf16[16,768,256]{2,1,0:T(8,128)(2,1)} custom-call(s32[2]{0:T(128)} %pad_add_fusion.place_ref, s32[16]{0:T(128)} %counts_ref.3, s32[3,16]{1,0:T(4,128)} %bitcast.12, bf16[2,16,16,4096]{3,2,1,0:T(8,128)(2,1)} %bitcast.8, bf16[2,3,256,256]{3,2,1,0:T(8,128)(2,1)} %bitcast.10, bf16[2,256]{1,0:T(2,128)(2,1)} %bitcast.15), custom_call_target="tpu_custom_call" | custom-call | flops 10000000 | bytes 10485760 | tf_op jit(solution)/shard_map/pallas_call | solution.py:76
  13.1 81.4 %all_to_all.10.spread_hbm = bf16[16,768,256]{2,1,0:T(8,128)(2,1)} all-to-all(bf16[16,768,256]{2,1,0:T(8,128)(2,1)} %shard_map.55), channel_id=1, replica_groups=mesh['occ'=8,'vir'=16] {'vir'}, dimensions={0} | all-to-all | bytes 12582912 | tf_op jit(solution)/shard_map/all_to_all | solution.py:326
  94.5 8.9 %shard_map.56 = (bf16[16,1024,256]{2,1,0:T(8,128)(2,1)}, bf16[3200,256]{1,0:T(8,128)(2,1)}) custom-call(s32[3,16]{1,0:T(4,128)} %bitcast.13, bf16[16,768,256]{2,1,0:T(8,128)(2,1)} %all_to_all.10.spread_hbm), custom_call_target="tpu_custom_call" | custom-call | bytes 20971520 | tf_op jit(solution)/shard_map/pallas_call | solution.py:150
  103.4 0.0 all-gather.3.cloned.1.call-update
  103.4 100.6 %all_to_all.11.fetched_hbm = bf16[16,1024,256]{2,1,0:T(8,128)(2,1)} all-to-all(bf16[16,1024,256]{2,1,0:T(8,128)(2,1)} %get-tuple-element.7), channel_id=1, replica_groups=mesh['occ'=8,'vir'=16] {'vir'}, dimensions={0} | all-to-all | bytes 16777216 | tf_op jit(solution)/shard_map/all_to_all | solution.py:329
  204.1 0.0 all-gather.3.cloned.1.call-done
  204.1 20.2 %shard_map.57 = bf16[512,4096]{1,0:T(8,128)(2,1)} custom-call(s32[3,16]{1,0:T(4,128)} %bitcast.14, s32[16]{0:T(128)} %counts_ref.3, s32[2]{0:T(128)} %pad_add_fusion.place_ref, bf16[2,16,16,4096]{3,2,1,0:T(8,128)(2,1)} %bitcast.9, bf16[16,1024,256]{2,1,0:T(8,128)(2,1)} %all_to_all.11.fetched_hbm, bf16[8,3200,256]{2,1,0:T(8,128)(2,1)} %bitcast.17, ...), custom_call_target="tpu_custom_call" | custom-call | flops 12000000000 | bytes 31457280 | tf_op jit(solution)/shard_map/pallas_call | solution.py:286
Async XLA Ops:
  6.5 197.5 %all-gather.3.cloned.1.call-start = ((), (), s32[]{:S(2)}) async-start(), calls=%async_computation.2 | async-start | bytes 14745600 | tf_op jit(solution)/shard_map/all_gather | solution.py:328
Sparse Core Ops, SparseCore 0:
  103.6 67.2 all-gather.2

commit v4 on v3

--- a/solution.py
+++ b/solution.py
@@ -32,9 +32,9 @@
         source = held_ref.at[index, :, :, pl.ds(column * tile, tile)]
         return pltpu.make_async_copy(source, chunks_hbm.at[:, place, :], out_sems.at[index, column])
 
-    def send(chunk):
-        place = pl.ds(partners * tile, same_ref.shape[0])
-        return pltpu.make_async_copy(same_ref, chunks_hbm.at[chunk, place, :], same_sems.at[chunk])
+    def send(chunk, first, rows, index):
+        place = pl.ds(partners * tile + first, rows)
+        return pltpu.make_async_copy(same_ref.at[pl.ds(first, rows), :], chunks_hbm.at[chunk, place, :], same_sems.at[index, chunk])
 
     for index in range(partners):
         load(index).start()
@@ -46,6 +46,8 @@
             live = (slot < count).astype(jnp.float32).astype(jnp.bfloat16)
             at = lines + (aux * slot_count + slot) * part
             same_ref[at : at + part, :] = own_ints_ref[aux, slot, pl.ds(first, part), :] * live
+    for chunk in range(chunk_count):
+        send(chunk, lines, same_ref.shape[0] - lines, 0).start()
 
     for index in range(partners):
         load(index).wait()
@@ -59,12 +61,13 @@
                 total_ref[line : line + 1, :] = total[aux : aux + 1]
     same_ref[:lines, :] = total_ref[...].astype(jnp.bfloat16)
     for chunk in range(chunk_count):
-        send(chunk).start()
+        send(chunk, 0, lines, 1).start()
     for index in range(partners):
         for column in range(columns):
             store(index, column).wait()
     for chunk in range(chunk_count):
-        send(chunk).wait()
+        send(chunk, lines, same_ref.shape[0] - lines, 0).wait()
+        send(chunk, 0, lines, 1).wait()
 
 
 def stage(place, counts, cols, amps, own_ints, left, parts):
@@ -84,7 +87,7 @@
             pltpu.VMEM((same, tile), amps.dtype),
             pltpu.SemaphoreType.DMA((partners,)),
             pltpu.SemaphoreType.DMA((partners, columns)),
-            pltpu.SemaphoreType.DMA((chunk_count,)),
+            pltpu.SemaphoreType.DMA((2, chunk_count)),
         ],
         compiler_params=pltpu.CompilerParams(vmem_limit_bytes=60 * MIB),
         cost_estimate=pl.CostEstimate(flops=10**7, bytes_accessed=10 * MIB, transcendentals=0),
@@ -92,17 +95,17 @@
 
 
 def pick_kernel(partners, cols_ref, spread_hbm, out_hbm, shared_hbm, held_ref, sums_ref, shared_ref, in_sems, out_sems, part_sems, sems):
-    chunks, slots = in_sems.shape
+    chunks, slots = out_sems.shape
     lines = sums_ref.shape[1]
-    rows = held_ref.shape[1] // slots
+    rows = held_ref.shape[1]
     part = spread_hbm.shape[1] - rows - lines
 
-    def fetch(chunk, slot):
-        source = spread_hbm.at[cols_ref[slot + 1, chunk], pl.ds(0, rows), :]
-        return pltpu.make_async_copy(source, held_ref.at[chunk, pl.ds(slot * rows, rows), :], in_sems.at[chunk, slot])
-
-    def store(chunk):
-        return pltpu.make_async_copy(held_ref.at[chunk], out_hbm.at[chunk], out_sems.at[chunk])
+    def fetch(chunk):
+        return pltpu.make_async_copy(spread_hbm.at[chunk, pl.ds(0, rows), :], held_ref.at[chunk], in_sems.at[chunk])
+
+    def store(chunk, slot):
+        place = out_hbm.at[chunk, pl.ds(slot * rows, rows), :]
+        return pltpu.make_async_copy(held_ref.at[cols_ref[slot + 1, chunk]], place, out_sems.at[chunk, slot])
 
     def part_copy(chunk):
         source = spread_hbm.at[chunk, pl.ds(rows + lines, part), :]
@@ -112,12 +115,9 @@
     shared_out = pltpu.make_async_copy(shared_ref, shared_hbm, sems.at[1])
     sums_in.start()
     for chunk in range(chunks):
+        fetch(chunk).start()
+    for chunk in range(chunks):
         part_copy(chunk).start()
-
-    @pl.loop(0, chunks)
-    def _(chunk):
-        for slot in range(slots):
-            fetch(chunk, slot).start()
 
     sums_in.wait()
     total = jnp.sum(sums_ref[...].astype(jnp.float32), axis=0)
@@ -125,18 +125,21 @@
     shared_ref[chunks * part : chunks * part + lines, :] = value
     shared_ref[chunks * part + lines :, :] = (total - value.astype(jnp.float32)).astype(jnp.bfloat16)
     for chunk in range(chunks):
+        fetch(chunk).wait()
+
+    @pl.loop(0, chunks)
+    def _(chunk):
+        for slot in range(slots):
+            store(chunk, slot).start()
+
+    for chunk in range(chunks):
         part_copy(chunk).wait()
     shared_out.start()
 
     @pl.loop(0, chunks)
     def _(chunk):
         for slot in range(slots):
-            fetch(chunk, slot).wait()
-        store(chunk).start()
-
-    @pl.loop(0, chunks)
-    def _(chunk):
-        store(chunk).wait()
+            store(chunk, slot).wait()
 
     shared_out.wait()
 
@@ -153,11 +156,11 @@
         out_specs=[HBM, HBM],
         out_shape=[jax.ShapeDtypeStruct(shape, spread.dtype), jax.ShapeDtypeStruct(shared, spread.dtype)],
         scratch_shapes=[
-            pltpu.VMEM(shape, spread.dtype),
+            pltpu.VMEM((chunks, partners * tile, tile), spread.dtype),
             pltpu.VMEM((chunks, lines, tile), spread.dtype),
             pltpu.VMEM(shared, spread.dtype),
+            pltpu.SemaphoreType.DMA((chunks,)),
             pltpu.SemaphoreType.DMA((chunks, slots - 1)),
-            pltpu.SemaphoreType.DMA((chunks,)),
             pltpu.SemaphoreType.DMA((chunks,)),
             pltpu.SemaphoreType.DMA((2,)),
         ],

time: 231 us -> 231 us (level)
  no operation moved by 1% of the time
where the time goes in v4:
time: 231 us; the launch traced here: 230 us
  blocking collectives  182 us (79%)
  Pallas kernels  34.1 us (15%)
  between operations  13.4 us (6%)
    all_to_all x1, blocking collectives, body(): lax.all_to_all(picked, 'vir', split_axis=0, concat_axis=0, tiled=True)  101 us
    all_to_all x1, blocking collectives, body(): lax.all_to_all(chunks, 'vir', split_axis=0, concat_axis=0, tiled=True)  81.4 us
    pallas_call x1, Pallas kernels, ladder(): pl.pallas_call(ladder_kernel, in_specs=[SMEM] * 3 + [HBM] * 3 + [VMEM] *...  20.2 us
    pallas_call x1, Pallas kernels, pick(): pl.pallas_call(functools.partial(pick_kernel, partners), in_specs=[SMEM,...  7.86 us
    pallas_call x1, Pallas kernels, stage(): pl.pallas_call(stage_kernel, in_specs=[SMEM, SMEM, SMEM, HBM, VMEM, VMEM]...  6.05 us
  transfers between devices with their start and end apart: 1, of which 0 were waited for; matrix products, arithmetic and copies ran while one was open for 0% of the time, Pallas kernels for 0%

profile of v4, /device:TPU:0, one launch (start us, length us, event | category | flops | bytes accessed | tf_op | source)
XLA Modules:
  0.0 230.2 jit_solution(3764083767557779386)
XLA Ops:
  6.5 0.0 all-gather.3.cloned.1.call-start
  6.5 0.6 pad_add_fusion.place_ref
  7.2 6.1 %shard_map.55 = bf16[16,768,256]{2,1,0:T(8,128)(2,1)} custom-call(s32[2]{0:T(128)} %pad_add_fusion.place_ref, s32[16]{0:T(128)} %counts_ref.3, s32[3,16]{1,0:T(4,128)} %bitcast.12, bf16[2,16,16,4096]{3,2,1,0:T(8,128)(2,1)} %bitcast.8, bf16[2,3,256,256]{3,2,1,0:T(8,128)(2,1)} %bitcast.10, bf16[2,256]{1,0:T(2,128)(2,1)} %bitcast.15), custom_call_target="tpu_custom_call" | custom-call | flops 10000000 | bytes 10485760 | tf_op jit(solution)/shard_map/pallas_call | solution.py:79
  13.2 81.4 %all_to_all.10.spread_hbm = bf16[16,768,256]{2,1,0:T(8,128)(2,1)} all-to-all(bf16[16,768,256]{2,1,0:T(8,128)(2,1)} %shard_map.55), channel_id=1, replica_groups=mesh['occ'=8,'vir'=16] {'vir'}, dimensions={0} | all-to-all | bytes 12582912 | tf_op jit(solution)/shard_map/all_to_all | solution.py:329
  94.6 7.9 %shard_map.56 = (bf16[16,1024,256]{2,1,0:T(8,128)(2,1)}, bf16[3200,256]{1,0:T(8,128)(2,1)}) custom-call(s32[3,16]{1,0:T(4,128)} %bitcast.13, bf16[16,768,256]{2,1,0:T(8,128)(2,1)} %all_to_all.10.spread_hbm), custom_call_target="tpu_custom_call" | custom-call | bytes 20971520 | tf_op jit(solution)/shard_map/pallas_call | solution.py:153
  102.5 0.0 all-gather.3.cloned.1.call-update
  102.5 100.6 %all_to_all.11.fetched_hbm = bf16[16,1024,256]{2,1,0:T(8,128)(2,1)} all-to-all(bf16[16,1024,256]{2,1,0:T(8,128)(2,1)} %get-tuple-element.7), channel_id=1, replica_groups=mesh['occ'=8,'vir'=16] {'vir'}, dimensions={0} | all-to-all | bytes 16777216 | tf_op jit(solution)/shard_map/all_to_all | solution.py:332
  203.2 0.0 all-gather.3.cloned.1.call-done
  203.2 20.2 %shard_map.57 = bf16[512,4096]{1,0:T(8,128)(2,1)} custom-call(s32[3,16]{1,0:T(4,128)} %bitcast.14, s32[16]{0:T(128)} %counts_ref.3, s32[2]{0:T(128)} %pad_add_fusion.place_ref, bf16[2,16,16,4096]{3,2,1,0:T(8,128)(2,1)} %bitcast.9, bf16[16,1024,256]{2,1,0:T(8,128)(2,1)} %all_to_all.11.fetched_hbm, bf16[8,3200,256]{2,1,0:T(8,128)(2,1)} %bitcast.17, ...), custom_call_target="tpu_custom_call" | custom-call | flops 12000000000 | bytes 31457280 | tf_op jit(solution)/shard_map/pallas_call | solution.py:289
Async XLA Ops:
  6.5 196.6 %all-gather.3.cloned.1.call-start = ((), (), s32[]{:S(2)}) async-start(), calls=%async_computation.2 | async-start | bytes 14745600 | tf_op jit(solution)/shard_map/all_gather | solution.py:331
Sparse Core Ops, SparseCore 0:
  102.7 67.2 all-gather.2

commit v5 on v4

--- a/solution.py
+++ b/solution.py
@@ -9,6 +9,9 @@
 
 ROW_CHUNKS = 4
 INT_CHUNKS = 4
+AHEAD = 1
+INTS_FROM = 2
+INT_STEP = INT_CHUNKS // (ROW_CHUNKS - INTS_FROM)
 MIB = 2**20
 HBM = pl.BlockSpec(memory_space=pltpu.HBM)
 VMEM = pl.BlockSpec(memory_space=pltpu.VMEM)
@@ -204,14 +207,14 @@
 
     cycle_copy = pltpu.make_async_copy(ints_hbm.at[:, pl.ds(held, 2 * lines), :], cycle_ref, cycle_sem)
 
-    for chunk in range(ROW_CHUNKS):
+    def start_rows(chunk):
         for partner in range(partners):
             near_copy(partner, chunk).start()
             for slot in range(slot_count - 1):
                 far_copy(partner, slot, chunk).start()
-    cycle_copy.start()
-    for chunk in range(INT_CHUNKS):
-        int_copy(chunk).start()
+
+    for chunk in range(AHEAD):
+        start_rows(chunk)
 
     count = counts_ref[place_ref[0]]
     for aux in range(aux_count):
@@ -230,6 +233,20 @@
             near_copy(partner, chunk).wait()
             for slot in range(slot_count - 1):
                 far_copy(partner, slot, chunk).wait()
+
+        @pl.when(chunk + AHEAD < ROW_CHUNKS)
+        def _():
+            start_rows(chunk + AHEAD)
+
+        @pl.when(chunk == INTS_FROM)
+        def _():
+            cycle_copy.start()
+
+        @pl.when(chunk >= INTS_FROM)
+        def _():
+            for index in range(INT_STEP):
+                int_copy((chunk - INTS_FROM) * INT_STEP + index).start()
+
         for piece in range(per_chunk):
             column = chunk * per_chunk + piece
             span = pl.ds(pl.multiple_of(column * tile, tile), tile)

time: 231 us -> 230 us (level)
  no operation moved by 1% of the time
where the time goes in v5:
time: 230 us; the launch traced here: 229 us
  blocking collectives  182 us (79%)
  Pallas kernels  33.3 us (14%)
  between operations  13.4 us (6%)
    all_to_all x1, blocking collectives, body(): lax.all_to_all(picked, 'vir', split_axis=0, concat_axis=0, tiled=True)  101 us
    all_to_all x1, blocking collectives, body(): lax.all_to_all(chunks, 'vir', split_axis=0, concat_axis=0, tiled=True)  81.4 us
    pallas_call x1, Pallas kernels, ladder(): pl.pallas_call(ladder_kernel, in_specs=[SMEM] * 3 + [HBM] * 3 + [VMEM] *...  19.4 us
    pallas_call x1, Pallas kernels, pick(): pl.pallas_call(functools.partial(pick_kernel, partners), in_specs=[SMEM,...  7.86 us
    pallas_call x1, Pallas kernels, stage(): pl.pallas_call(stage_kernel, in_specs=[SMEM, SMEM, SMEM, HBM, VMEM, VMEM]...  6.05 us
  transfers between devices with their start and end apart: 1, of which 0 were waited for; matrix products, arithmetic and copies ran while one was open for 0% of the time, Pallas kernels for 0%

profile of v5, /device:TPU:0, one launch (start us, length us, event | category | flops | bytes accessed | tf_op | source)
XLA Modules:
  0.0 229.5 jit_solution(9230108014320124752)
XLA Ops:
  6.5 0.0 all-gather.3.cloned.1.call-start
  6.5 0.6 pad_add_fusion.place_ref
  7.2 6.1 %shard_map.55 = bf16[16,768,256]{2,1,0:T(8,128)(2,1)} custom-call(s32[2]{0:T(128)} %pad_add_fusion.place_ref, s32[16]{0:T(128)} %counts_ref.3, s32[3,16]{1,0:T(4,128)} %bitcast.12, bf16[2,16,16,4096]{3,2,1,0:T(8,128)(2,1)} %bitcast.8, bf16[2,3,256,256]{3,2,1,0:T(8,128)(2,1)} %bitcast.10, bf16[2,256]{1,0:T(2,128)(2,1)} %bitcast.15), custom_call_target="tpu_custom_call" | custom-call | flops 10000000 | bytes 10485760 | tf_op jit(solution)/shard_map/pallas_call | solution.py:82
  13.2 81.4 %all_to_all.10.spread_hbm = bf16[16,768,256]{2,1,0:T(8,128)(2,1)} all-to-all(bf16[16,768,256]{2,1,0:T(8,128)(2,1)} %shard_map.55), channel_id=1, replica_groups=mesh['occ'=8,'vir'=16] {'vir'}, dimensions={0} | all-to-all | bytes 12582912 | tf_op jit(solution)/shard_map/all_to_all | solution.py:346
  94.6 7.9 %shard_map.56 = (bf16[16,1024,256]{2,1,0:T(8,128)(2,1)}, bf16[3200,256]{1,0:T(8,128)(2,1)}) custom-call(s32[3,16]{1,0:T(4,128)} %bitcast.13, bf16[16,768,256]{2,1,0:T(8,128)(2,1)} %all_to_all.10.spread_hbm), custom_call_target="tpu_custom_call" | custom-call | bytes 20971520 | tf_op jit(solution)/shard_map/pallas_call | solution.py:156
  102.5 0.0 all-gather.3.cloned.1.call-update
  102.5 100.6 %all_to_all.11.fetched_hbm = bf16[16,1024,256]{2,1,0:T(8,128)(2,1)} all-to-all(bf16[16,1024,256]{2,1,0:T(8,128)(2,1)} %get-tuple-element.7), channel_id=1, replica_groups=mesh['occ'=8,'vir'=16] {'vir'}, dimensions={0} | all-to-all | bytes 16777216 | tf_op jit(solution)/shard_map/all_to_all | solution.py:349
  203.2 0.0 all-gather.3.cloned.1.call-done
  203.2 19.4 %shard_map.57 = bf16[512,4096]{1,0:T(8,128)(2,1)} custom-call(s32[3,16]{1,0:T(4,128)} %bitcast.14, s32[16]{0:T(128)} %counts_ref.3, s32[2]{0:T(128)} %pad_add_fusion.place_ref, bf16[2,16,16,4096]{3,2,1,0:T(8,128)(2,1)} %bitcast.9, bf16[16,1024,256]{2,1,0:T(8,128)(2,1)} %all_to_all.11.fetched_hbm, bf16[8,3200,256]{2,1,0:T(8,128)(2,1)} %bitcast.17, ...), custom_call_target="tpu_custom_call" | custom-call | flops 12000000000 | bytes 31457280 | tf_op jit(solution)/shard_map/pallas_call | solution.py:306
Async XLA Ops:
  6.5 196.6 %all-gather.3.cloned.1.call-start = ((), (), s32[]{:S(2)}) async-start(), calls=%async_computation.2 | async-start | bytes 14745600 | tf_op jit(solution)/shard_map/all_gather | solution.py:348
Sparse Core Ops, SparseCore 0:
  102.7 67.2 all-gather.2

commit v6 on v5

--- a/solution.py
+++ b/solution.py
@@ -7,6 +7,7 @@
 from jax.experimental.pallas import tpu as pltpu
 from jax.sharding import PartitionSpec as P
 
+LOADS = 4
 ROW_CHUNKS = 4
 INT_CHUNKS = 4
 AHEAD = 1
@@ -27,8 +28,14 @@
     lines = total_ref.shape[0]
     part = (same_ref.shape[0] - lines) // (aux_count * slot_count)
 
-    def load(index):
-        return pltpu.make_async_copy(amps_hbm.at[index], held_ref.at[index], in_sems.at[index])
+    pieces = in_sems.shape[1]
+    wide = virtuals // pieces
+
+    def load(index, piece):
+        span = pl.ds(piece * wide, wide)
+        return pltpu.make_async_copy(
+            amps_hbm.at[index, :, :, span], held_ref.at[index, :, :, span], in_sems.at[index, piece]
+        )
 
     def store(index, column):
         place = pl.ds((index * columns + column) * chunk_rows, chunk_rows)
@@ -40,7 +47,8 @@
         return pltpu.make_async_copy(same_ref.at[pl.ds(first, rows), :], chunks_hbm.at[chunk, place, :], same_sems.at[index, chunk])
 
     for index in range(partners):
-        load(index).start()
+        for piece in range(pieces):
+            load(index, piece).start()
 
     count = counts_ref[place_ref[0]]
     first = pl.multiple_of(place_ref[1] * part, part)
@@ -53,9 +61,10 @@
         send(chunk, lines, same_ref.shape[0] - lines, 0).start()
 
     for index in range(partners):
-        load(index).wait()
-        for column in range(columns):
-            store(index, column).start()
+        for piece in range(pieces):
+            load(index, piece).wait()
+            for column in range(piece * columns // pieces, (piece + 1) * columns // pieces):
+                store(index, column).start()
         for column in range(columns):
             rows = held_ref[index, :, :, column * tile : (column + 1) * tile].reshape(tile, tile)
             total = jnp.dot(left_ref[...], rows, preferred_element_type=jnp.float32)
@@ -88,7 +97,7 @@
             pltpu.VMEM(amps.shape, amps.dtype),
             pltpu.VMEM((lines, tile), jnp.float32),
             pltpu.VMEM((same, tile), amps.dtype),
-            pltpu.SemaphoreType.DMA((partners,)),
+            pltpu.SemaphoreType.DMA((partners, LOADS)),
             pltpu.SemaphoreType.DMA((partners, columns)),
             pltpu.SemaphoreType.DMA((2, chunk_count)),
         ],

time: 230 us -> 230 us (level)
  no operation moved by 1% of the time
where the time goes in v6:
time: 230 us
  blocking collectives  182 us (79%)
  Pallas kernels  33.8 us (15%)
  between operations  13.4 us (6%)
    all_to_all x1, blocking collectives, body(): lax.all_to_all(picked, 'vir', split_axis=0, concat_axis=0, tiled=True)  101 us
    all_to_all x1, blocking collectives, body(): lax.all_to_all(chunks, 'vir', split_axis=0, concat_axis=0, tiled=True)  81.4 us
    pallas_call x1, Pallas kernels, ladder(): pl.pallas_call(ladder_kernel, in_specs=[SMEM] * 3 + [HBM] * 3 + [VMEM] *...  19.4 us
    pallas_call x1, Pallas kernels, pick(): pl.pallas_call(functools.partial(pick_kernel, partners), in_specs=[SMEM,...  7.86 us
    pallas_call x1, Pallas kernels, stage(): pl.pallas_call(stage_kernel, in_specs=[SMEM, SMEM, SMEM, HBM, VMEM, VMEM]...  6.54 us
  transfers between devices with their start and end apart: 1, of which 0 were waited for; matrix products, arithmetic and copies ran while one was open for 0% of the time, Pallas kernels for 0%

profile of v6, /device:TPU:0, one launch (start us, length us, event | category | flops | bytes accessed | tf_op | source)
XLA Modules:
  0.0 230.0 jit_solution(6103014948480738656)
XLA Ops:
  6.5 0.0 all-gather.3.cloned.1.call-start
  6.5 0.6 pad_add_fusion.place_ref
  7.2 6.5 %shard_map.55 = bf16[16,768,256]{2,1,0:T(8,128)(2,1)} custom-call(s32[2]{0:T(128)} %pad_add_fusion.place_ref, s32[16]{0:T(128)} %counts_ref.3, s32[3,16]{1,0:T(4,128)} %bitcast.12, bf16[2,16,16,4096]{3,2,1,0:T(8,128)(2,1)} %bitcast.8, bf16[2,3,256,256]{3,2,1,0:T(8,128)(2,1)} %bitcast.10, bf16[2,256]{1,0:T(2,128)(2,1)} %bitcast.15), custom_call_target="tpu_custom_call" | custom-call | flops 10000000 | bytes 10485760 | tf_op jit(solution)/shard_map/pallas_call | solution.py:91
  13.7 81.4 %all_to_all.10.spread_hbm = bf16[16,768,256]{2,1,0:T(8,128)(2,1)} all-to-all(bf16[16,768,256]{2,1,0:T(8,128)(2,1)} %shard_map.55), channel_id=1, replica_groups=mesh['occ'=8,'vir'=16] {'vir'}, dimensions={0} | all-to-all | bytes 12582912 | tf_op jit(solution)/shard_map/all_to_all | solution.py:355
  95.1 7.9 %shard_map.56 = (bf16[16,1024,256]{2,1,0:T(8,128)(2,1)}, bf16[3200,256]{1,0:T(8,128)(2,1)}) custom-call(s32[3,16]{1,0:T(4,128)} %bitcast.13, bf16[16,768,256]{2,1,0:T(8,128)(2,1)} %all_to_all.10.spread_hbm), custom_call_target="tpu_custom_call" | custom-call | bytes 20971520 | tf_op jit(solution)/shard_map/pallas_call | solution.py:165
  103.0 0.0 all-gather.3.cloned.1.call-update
  103.0 100.6 %all_to_all.11.fetched_hbm = bf16[16,1024,256]{2,1,0:T(8,128)(2,1)} all-to-all(bf16[16,1024,256]{2,1,0:T(8,128)(2,1)} %get-tuple-element.7), channel_id=1, replica_groups=mesh['occ'=8,'vir'=16] {'vir'}, dimensions={0} | all-to-all | bytes 16777216 | tf_op jit(solution)/shard_map/all_to_all | solution.py:358
  203.7 0.0 all-gather.3.cloned.1.call-done
  203.7 19.4 %shard_map.57 = bf16[512,4096]{1,0:T(8,128)(2,1)} custom-call(s32[3,16]{1,0:T(4,128)} %bitcast.14, s32[16]{0:T(128)} %counts_ref.3, s32[2]{0:T(128)} %pad_add_fusion.place_ref, bf16[2,16,16,4096]{3,2,1,0:T(8,128)(2,1)} %bitcast.9, bf16[16,1024,256]{2,1,0:T(8,128)(2,1)} %all_to_all.11.fetched_hbm, bf16[8,3200,256]{2,1,0:T(8,128)(2,1)} %bitcast.17, ...), custom_call_target="tpu_custom_call" | custom-call | flops 12000000000 | bytes 31457280 | tf_op jit(solution)/shard_map/pallas_call | solution.py:315
Async XLA Ops:
  6.5 197.1 %all-gather.3.cloned.1.call-start = ((), (), s32[]{:S(2)}) async-start(), calls=%async_computation.2 | async-start | bytes 14745600 | tf_op jit(solution)/shard_map/all_gather | solution.py:357
Sparse Core Ops, SparseCore 0:
  103.1 67.2 all-gather.2

commit v7 on v5

--- a/solution.py
+++ b/solution.py
@@ -119,8 +119,6 @@
     sums_in.start()
     for chunk in range(chunks):
         fetch(chunk).start()
-    for chunk in range(chunks):
-        part_copy(chunk).start()
 
     sums_in.wait()
     total = jnp.sum(sums_ref[...].astype(jnp.float32), axis=0)
@@ -129,6 +127,9 @@
     shared_ref[chunks * part + lines :, :] = (total - value.astype(jnp.float32)).astype(jnp.bfloat16)
     for chunk in range(chunks):
         fetch(chunk).wait()
+
+    for chunk in range(chunks):
+        part_copy(chunk).start()
 
     @pl.loop(0, chunks)
     def _(chunk):

time: 230 us -> 230 us (level)
  no operation moved by 1% of the time
where the time goes in v7:
time: 230 us; the launch traced here: 229 us
  blocking collectives  182 us (79%)
  Pallas kernels  33.1 us (14%)
  between operations  13.4 us (6%)
    all_to_all x1, blocking collectives, body(): lax.all_to_all(picked, 'vir', split_axis=0, concat_axis=0, tiled=True)  101 us
    all_to_all x1, blocking collectives, body(): lax.all_to_all(chunks, 'vir', split_axis=0, concat_axis=0, tiled=True)  81.4 us
    pallas_call x1, Pallas kernels, ladder(): pl.pallas_call(ladder_kernel, in_specs=[SMEM] * 3 + [HBM] * 3 + [VMEM] *...  19.4 us
    pallas_call x1, Pallas kernels, pick(): pl.pallas_call(functools.partial(pick_kernel, partners), in_specs=[SMEM,...  7.57 us
    pallas_call x1, Pallas kernels, stage(): pl.pallas_call(stage_kernel, in_specs=[SMEM, SMEM, SMEM, HBM, VMEM, VMEM]...  6.05 us
  transfers between devices with their start and end apart: 1, of which 0 were waited for; matrix products, arithmetic and copies ran while one was open for 0% of the time, Pallas kernels for 0%

profile of v7, /device:TPU:0, one launch (start us, length us, event | category | flops | bytes accessed | tf_op | source)
XLA Modules:
  0.0 229.2 jit_solution(9731819878168717645)
XLA Ops:
  6.5 0.0 all-gather.3.cloned.1.call-start
  6.5 0.6 pad_add_fusion.place_ref
  7.2 6.1 %shard_map.55 = bf16[16,768,256]{2,1,0:T(8,128)(2,1)} custom-call(s32[2]{0:T(128)} %pad_add_fusion.place_ref, s32[16]{0:T(128)} %counts_ref.3, s32[3,16]{1,0:T(4,128)} %bitcast.12, bf16[2,16,16,4096]{3,2,1,0:T(8,128)(2,1)} %bitcast.8, bf16[2,3,256,256]{3,2,1,0:T(8,128)(2,1)} %bitcast.10, bf16[2,256]{1,0:T(2,128)(2,1)} %bitcast.15), custom_call_target="tpu_custom_call" | custom-call | flops 10000000 | bytes 10485760 | tf_op jit(solution)/shard_map/pallas_call | solution.py:82
  13.2 81.4 %all_to_all.10.spread_hbm = bf16[16,768,256]{2,1,0:T(8,128)(2,1)} all-to-all(bf16[16,768,256]{2,1,0:T(8,128)(2,1)} %shard_map.55), channel_id=1, replica_groups=mesh['occ'=8,'vir'=16] {'vir'}, dimensions={0} | all-to-all | bytes 12582912 | tf_op jit(solution)/shard_map/all_to_all | solution.py:347
  94.6 7.6 %shard_map.56 = (bf16[16,1024,256]{2,1,0:T(8,128)(2,1)}, bf16[3200,256]{1,0:T(8,128)(2,1)}) custom-call(s32[3,16]{1,0:T(4,128)} %bitcast.13, bf16[16,768,256]{2,1,0:T(8,128)(2,1)} %all_to_all.10.spread_hbm), custom_call_target="tpu_custom_call" | custom-call | bytes 20971520 | tf_op jit(solution)/shard_map/pallas_call | solution.py:157
  102.2 0.0 all-gather.3.cloned.1.call-update
  102.2 100.6 %all_to_all.11.fetched_hbm = bf16[16,1024,256]{2,1,0:T(8,128)(2,1)} all-to-all(bf16[16,1024,256]{2,1,0:T(8,128)(2,1)} %get-tuple-element.7), channel_id=1, replica_groups=mesh['occ'=8,'vir'=16] {'vir'}, dimensions={0} | all-to-all | bytes 16777216 | tf_op jit(solution)/shard_map/all_to_all | solution.py:350
  202.9 0.0 all-gather.3.cloned.1.call-done
  202.9 19.4 %shard_map.57 = bf16[512,4096]{1,0:T(8,128)(2,1)} custom-call(s32[3,16]{1,0:T(4,128)} %bitcast.14, s32[16]{0:T(128)} %counts_ref.3, s32[2]{0:T(128)} %pad_add_fusion.place_ref, bf16[2,16,16,4096]{3,2,1,0:T(8,128)(2,1)} %bitcast.9, bf16[16,1024,256]{2,1,0:T(8,128)(2,1)} %all_to_all.11.fetched_hbm, bf16[8,3200,256]{2,1,0:T(8,128)(2,1)} %bitcast.17, ...), custom_call_target="tpu_custom_call" | custom-call | flops 12000000000 | bytes 31457280 | tf_op jit(solution)/shard_map/pallas_call | solution.py:307
Async XLA Ops:
  6.5 196.3 %all-gather.3.cloned.1.call-start = ((), (), s32[]{:S(2)}) async-start(), calls=%async_computation.2 | async-start | bytes 14745600 | tf_op jit(solution)/shard_map/all_gather | solution.py:349
Sparse Core Ops, SparseCore 0:
  102.4 67.2 all-gather.2
